TPU v7x, 32 devices: a whole 2x2x4 slice. The times are simulated.
32 devices in a mesh: tm: 8 (over y, x, core), head: 4 (over z).
Axes of the slice: x: 2, y: 2, z: 4, core: 2. Of those that a mesh axis runs over, the one named last changes fastest.
Arguments:
- frames: bfloat16 [32768, 144], P(('tm', 'head')), may hold values from -6 to 6
- lengths: int32 [8, 165], P('tm'), may hold values from 0 to 750, as said below
- first_gain: bfloat16 [144], replicated, may hold values from 0.25 to 1.75
- first_shift: bfloat16 [144], replicated, may hold values from -1.25 to 1.25
- first_up: bfloat16 [144, 576], replicated, may hold values from -0.5 to 0.5
- first_up_bias: bfloat16 [576], replicated, may hold values from -1.25 to 1.25
- first_down: bfloat16 [576, 144], replicated, may hold values from -0.25 to 0.25
- first_down_bias: bfloat16 [144], replicated, may hold values from -1.25 to 1.25
- mix_gain: bfloat16 [144], replicated, may hold values from 0.25 to 1.75
- mix_shift: bfloat16 [144], replicated, may hold values from -1.25 to 1.25
- mix_inputs: bfloat16 [144, 432], replicated, may hold values from -0.5 to 0.5
- position_bias: bfloat16 [4, 128], replicated, may hold values from -3 to 3
- mix_output: bfloat16 [144, 144], replicated, may hold values from -3 to 3
- mix_output_bias: bfloat16 [144], replicated, may hold values from -1.25 to 1.25
- filter_gain: bfloat16 [144], replicated, may hold values from 0.25 to 1.75
- filter_shift: bfloat16 [144], replicated, may hold values from -1.25 to 1.25
- pointwise_in: bfloat16 [144, 288], replicated, may hold values from -0.5 to 0.5
- pointwise_in_bias: bfloat16 [288], replicated, may hold values from -1.25 to 1.25
- depthwise_taps: bfloat16 [32, 144], replicated, may hold values from -1 to 1
- batch_gain: bfloat16 [144], replicated, may hold values from 0.25 to 1.75
- batch_shift: bfloat16 [144], replicated, may hold values from -1.25 to 1.25
- pointwise_out: bfloat16 [144, 144], replicated, may hold values from -0.5 to 0.5
- pointwise_out_bias: bfloat16 [144], replicated, may hold values from -1.25 to 1.25
- second_gain: bfloat16 [144], replicated, may hold values from 0.25 to 1.75
- second_shift: bfloat16 [144], replicated, may hold values from -1.25 to 1.25
- second_up: bfloat16 [144, 576], replicated, may hold values from -0.5 to 0.5
- second_up_bias: bfloat16 [576], replicated, may hold values from -1.25 to 1.25
- second_down: bfloat16 [576, 144], replicated, may hold values from -0.25 to 0.25
- second_down_bias: bfloat16 [144], replicated, may hold values from -1.25 to 1.25
- final_gain: bfloat16 [144], replicated, may hold values from 0.25 to 1.75
- final_shift: bfloat16 [144], replicated, may hold values from -1.25 to 1.25
- cotangent: bfloat16 [32768, 144], P(('tm', 'head')), may hold values from -6 to 6
Outputs:
- layer_output: bfloat16 [32768, 144], P(('tm', 'head'))
- frames_grad: float32 [32768, 144], P(('tm', 'head'))
- grad_first_gain: float32 [144], replicated
- grad_first_shift: float32 [144], replicated
- grad_first_up: float32 [144, 576], replicated
- grad_first_up_bias: float32 [576], replicated
- grad_first_down: float32 [576, 144], replicated
- grad_first_down_bias: float32 [144], replicated
- grad_mix_gain: float32 [144], replicated
- grad_mix_shift: float32 [144], replicated
- grad_mix_inputs: float32 [144, 432], replicated
- grad_position_bias: float32 [4, 128], replicated
- grad_mix_output: float32 [144, 144], replicated
- grad_mix_output_bias: float32 [144], replicated
- grad_filter_gain: float32 [144], replicated
- grad_filter_shift: float32 [144], replicated
- grad_pointwise_in: float32 [144, 288], replicated
- grad_pointwise_in_bias: float32 [288], replicated
- grad_depthwise_taps: float32 [32, 144], replicated
- grad_batch_gain: float32 [144], replicated
- grad_batch_shift: float32 [144], replicated
- grad_pointwise_out: float32 [144, 144], replicated
- grad_pointwise_out_bias: float32 [144], replicated
- grad_second_gain: float32 [144], replicated
- grad_second_shift: float32 [144], replicated
- grad_second_up: float32 [144, 576], replicated
- grad_second_up_bias: float32 [576], replicated
- grad_second_down: float32 [576, 144], replicated
- grad_second_down_bias: float32 [144], replicated
- grad_final_gain: float32 [144], replicated
- grad_final_shift: float32 [144], replicated
Inputs may be any that keep to these rules, and one draw needn't show every extreme that they name: `lengths`: row g lists in order the utterances packed into group g from its first frame on; frames after the last utterance are padding, and slots after it are 0. Every row holds one utterance of 750 frames among its first two slots; the others have 25 to 75 frames, except the last one, which may be cut shorter. The last group has no padding.
All inputs are finite; a program needn't handle non-finite values.
Results may differ from a plain program's by a relative error of at most 0.017.
Values may be sent and summed in bfloat16 or wider, within the bound.
A program may use at most 128 MiB of HBM per device.

v0:
```python
import dataclasses
import functools
import math
import types

import jax
import jax.numpy as jnp
from jax import lax
from jax.experimental import pallas as pl
from jax.experimental.pallas import tpu as pltpu
from jax.sharding import PartitionSpec as P

BF = jnp.bfloat16
F32 = jnp.float32
LOG2E = math.log2(math.e)
BLK = 512
UNIT = 128
PER = BLK // UNIT
NEAR = PER + 2
PAD = 8 * UNIT
SLOT = 48
DEPTH = 128
MASKED = -1e30
GANG = 4
NN = (((1,), (0,)), ((), ()))
NT = (((1,), (1,)), ((), ()))
TN = (((0,), (0,)), ((), ()))


def dot(a, b, dims=NN):
    return lax.dot_general(a, b, dims, preferred_element_type=F32)


def iota(shape, dim):
    return lax.broadcasted_iota(jnp.int32, shape, dim)


def spread_cols(width, slots, slot_rows, used):
    row, column = iota((slots * slot_rows, width), 0), iota((slots * slot_rows, width), 1)
    hit = jnp.zeros((slots * slot_rows, width), jnp.bool_)
    for s in range(slots):
        f = row - slot_rows * s
        hit = hit | ((f >= 0) & (f < used) & (column == used * s + f))
    return hit.astype(F32).astype(BF)


def split3(v):
    hi = v.astype(BF).astype(F32)
    r1 = v - hi
    mid = r1.astype(BF).astype(F32)
    return hi, mid, r1 - mid


def three_rows(v, rows):
    a, b, e = split3(v)
    row = iota((rows, v.shape[1]), 0)
    return jnp.where(row == 0, a, jnp.where(row == 1, b, jnp.where(row == 2, e, 0.0)))


def pick_row(ref, index):
    values = ref[...].astype(F32)
    return jnp.sum(jnp.where(iota(values.shape, 0) == index, values, 0.0), axis=0, keepdims=True)


def bias_square(table, d):
    span = table.shape[1]
    half = span // 2
    lanes = 2 * UNIT
    u = iota((span, lanes), 1)
    u = jnp.where(u < UNIT, u, u - lanes)
    ids = jnp.clip(-UNIT * d - u, -half, half - 1) + half
    hot = (ids == iota((span, lanes), 0)).astype(F32).astype(BF)
    line = dot(jnp.broadcast_to(table, (UNIT, span)).astype(BF), hot) * LOG2E
    return pltpu.roll(line, 0, 1, stride=1, stride_axis=0)[:, :UNIT]


def bias_near(table, tile, keys_near):
    span = table.shape[1]
    squares = {d: bias_square(table, d) for d in (-1, 0, 1)}
    low = jnp.broadcast_to(table[:, :1] * LOG2E, (UNIT, UNIT))
    high = jnp.broadcast_to(table[:, span - 1 :] * LOG2E, (UNIT, UNIT))
    for r in range(tile.shape[0] // UNIT):
        for c in range(tile.shape[1] // UNIT):
            d = c - (r - 1) if keys_near else (c - 1) - r
            part = squares[d] if abs(d) < 2 else (low if d > 0 else high)
            tile[r * UNIT : (r + 1) * UNIT, c * UNIT : (c + 1) * UNIT] = part


def units_at(u, count):
    return pl.ds(pl.multiple_of(u * UNIT, UNIT), count * UNIT)


def far_windows(low, plain, edge, step, side, up, fine):
    sign = 1 if up else -1

    def run(at, times, size, masked):
        def one(i, carry):
            near = at + sign * i * size
            step(near if up else near - size, size, side, masked)
            return carry

        lax.fori_loop(0, times, one, 0)
        return at + sign * times * size

    at = edge if plain is None else run(edge, sign * (plain - edge) // 8, 8, False)
    left = sign * (low - at)
    tail = lax.rem(left, 8)
    more = tail > (6 if fine else 4)
    at = run(at, left // 8 + more.astype(jnp.int32), 8, True)
    tail = jnp.where(more, 0, tail)
    four = tail > (2 if fine else 0)
    at = run(at, four.astype(jnp.int32), 4, True)
    if fine:
        run(at, (tail - jnp.where(four, 4, 0) > 0).astype(jnp.int32), 2, True)


def far_sweep(plan, block, step, before, after, fine):
    low, plain_low, plain_high, high, low_half, high_half = [plan[block, i] for i in range(6)]
    start, stop = PER * block - 1, PER * block + PER + 1
    for whole, part in ((True, None), (False, 0)):
        @pl.when((low_half == 0) if whole else (low_half != 0))
        def _():
            far_windows(low, plain_low if whole else None, start, functools.partial(step, part=part), before, False, fine)

    for whole, part in ((True, None), (False, 1)):
        @pl.when((high_half == 0) if whole else (high_half != 0))
        def _():
            far_windows(high, plain_high if whole else None, stop, functools.partial(step, part=part), after, True, fine)


def part_at(block, part):
    if part is None:
        return units_at(PER * block, PER)
    return units_at(PER * block + part * (PER // 2), PER // 2)


def has_far(plan, block):
    return (plan[block, 0] < PER * block - 1) | (plan[block, 3] > PER * block + PER + 1)


def segment_rows(ends, lengths, place, total):
    slots = ends.shape[0]
    before = ends <= jnp.broadcast_to(place, (slots, place.shape[1]))
    seg = jnp.sum(before.astype(jnp.int32), axis=0, keepdims=True)
    first = jnp.sum(jnp.where(before, lengths, 0), axis=0, keepdims=True)
    stop = jnp.min(jnp.where(before, total, ends), axis=0, keepdims=True)
    return seg, first, stop


def block_plan(ends, ends_row, total):
    slots = ends.shape[0]
    blocks, units = total // BLK, total // UNIT

    def along(place):
        return jnp.sum((ends <= jnp.broadcast_to(place, (slots, 128))).astype(jnp.int32), axis=0, keepdims=True)

    def down(place):
        return jnp.sum((jnp.broadcast_to(ends_row, (blocks, slots)) <= place).astype(F32), axis=1, keepdims=True).astype(jnp.int32)

    unit = iota((1, 128), 1)
    u_first, u_last = along(unit * UNIT), along(unit * UNIT + UNIT - 1)
    b = iota((blocks, 1), 0)
    first, last = down(b * BLK), down(b * BLK + BLK - 1)
    low_half = (down(b * BLK + BLK // 2) != first).astype(jnp.int32)
    high_half = (down(b * BLK + BLK // 2 - 1) != last).astype(jnp.int32)
    start, stop = PER * b - 1, PER * b + PER + 1
    inside = unit < units

    def count(hit):
        return jnp.sum((hit & inside).astype(F32), axis=1, keepdims=True).astype(jnp.int32)

    low = jnp.minimum(count(u_last < first), start)
    high = jnp.maximum(units - count(u_first > last), stop)
    plain_low = start - count((unit < start) & (u_first == last))
    plain_high = stop + count((unit >= stop) & (u_last == first))
    lane = iota((blocks, 128), 1)
    out = jnp.zeros((blocks, 128), jnp.int32)
    for i, v in enumerate((low, plain_low, plain_high, high, low_half, high_half)):
        out = jnp.where(lane == i, v, out)
    return out


def meets(first_key, rows, bounds):
    key = iota((rows, bounds.shape[1]), 0)
    return (key >= bounds[0:1, :] - first_key) & (key < bounds[1:2, :] - first_key)


def fwd_kernel(plan, qkv_ref, table_ref, bound_ref, o_ref, of_ref, lse_ref, qaug, kn, vt, tile, top_ref, acc, *, head_width):
    chunks, packed_rows, rows = qkv_ref.shape
    total = chunks * rows
    blocks = total // BLK
    span = table_ref.shape[1]
    table = pick_row(table_ref, lax.axis_index("head"))
    far = (table[:, :1] * LOG2E, table[:, span - 1 :] * LOG2E)
    pick = spread_cols(packed_rows, 3, SLOT, head_width)
    scale = LOG2E / math.sqrt(head_width)
    o_ref[:, :UNIT] = jnp.zeros((SLOT, UNIT), BF)
    o_ref[:, UNIT + total :] = jnp.zeros((SLOT, UNIT), BF)
    for edge in (slice(0, PAD), slice(PAD + total, 2 * PAD + total)):
        kn[edge, :] = jnp.zeros((PAD, DEPTH), BF)
        vt[:, edge] = jnp.zeros((SLOT, PAD), BF)
    bias_near(table, tile, True)
    rest = DEPTH - 2 * SLOT

    @pl.loop(0, chunks)
    def _(c):
        at = pl.ds(pl.multiple_of(c * rows, rows), rows)
        at_pad = pl.ds(pl.multiple_of(c * rows + PAD, UNIT), rows)
        parts = dot(pick, qkv_ref[c])
        q = parts[:SLOT] * scale
        hi = q.astype(BF)
        lo = (q - hi.astype(F32)).astype(BF)
        for s in range(3):
            qaug[s, :SLOT, at] = hi
            qaug[s, SLOT : 2 * SLOT, at] = lo
            qaug[s, 2 * SLOT :, at] = jnp.zeros((rest, rows), BF)
        k = parts[SLOT : 2 * SLOT]
        one3 = (iota((rest, rows), 0) < 3).astype(F32)
        kn[at_pad, :] = jnp.concatenate([k, k, one3], axis=0).T.astype(BF)
        one = (iota((SLOT, rows), 0) == head_width).astype(F32)
        vt[:, at_pad] = (parts[2 * SLOT :] + one).astype(BF)

    def top(x):
        return jnp.max(x.reshape(x.shape[0] // 8, 8, BLK), axis=0)

    @pl.loop(0, blocks // GANG)
    def _(pair):
        blocks_now = [GANG * pair + i for i in range(GANG)]
        at_q = [units_at(PER * b, PER) for b in blocks_now]
        near = [units_at(PER * b - 1 + PAD // UNIT, NEAR) for b in blocks_now]
        x = [dot(kn[n, :], qaug[1, :, q]) + tile[...] for n, q in zip(near, at_q)]
        x = [
            jnp.where(meets(PER * b * UNIT - UNIT, NEAR * UNIT, bound_ref[:, units_at(PER * b + PAD // UNIT, PER)]), v, MASKED)
            for b, v in zip(blocks_now, x)
        ]
        m = [jnp.max(top(v), axis=0, keepdims=True) for v in x]
        p = [jnp.exp2(v - w).astype(BF) for v, w in zip(x, m)]
        out = [dot(vt[:, n], v) for n, v in zip(near, p)]
        for q, w, v in zip(at_q, m, out):
            acc[:, q] = v
            lse_ref[:, q] = w
            qaug[0, 2 * SLOT :, q] = three_rows(far[0] - w, rest).astype(BF)
            qaug[2, 2 * SLOT :, q] = three_rows(far[1] - w, rest).astype(BF)

    @pl.loop(0, blocks)
    def _(b):
        @pl.when(has_far(plan, b))
        def _():
            at_q = units_at(PER * b, PER)

            def scores(u, count, side, masked, part):
                x = dot(kn[units_at(u + PAD // UNIT, count), :], qaug[side, :, part_at(b, part)])
                if masked:
                    x = jnp.where(meets(u * UNIT, count * UNIT, bound_ref[:, part_at(b + PAD // BLK, part)]), x, MASKED)
                return x

            near_acc = acc[:, at_q]

            def add(u, count, side, masked, part):
                p = jnp.exp2(scores(u, count, side, masked, part)).astype(BF)
                acc[:, part_at(b, part)] += dot(vt[:, units_at(u + PAD // UNIT, count)], p)

            far_sweep(plan, b, add, 0, 2, False)
            sums = acc[head_width : head_width + 1, at_q]
            over = jnp.max(jnp.where(sums < 2.0**60, 0.0, 1.0))

            @pl.when(over > 0.5)
            def _():
                top_ref[...] = jnp.zeros_like(top_ref)

                def half_of(part):
                    return slice(None) if part is None else slice(part * BLK // 2, (part + 1) * BLK // 2)

                def first(u, count, side, masked, part):
                    x = scores(u, count, side, masked, part)
                    best = jnp.max(x.reshape(x.shape[0] // 8, 8, x.shape[1]), axis=0)
                    top_ref[:, half_of(part)] = jnp.maximum(top_ref[:, half_of(part)], best)

                far_sweep(plan, b, first, 0, 2, False)
                m = jnp.max(top_ref[...], axis=0, keepdims=True)
                acc[:, at_q] = near_acc * jnp.exp2(-m)
                lse_ref[:, at_q] += m

                def second(u, count, side, masked, part):
                    p = jnp.exp2(scores(u, count, side, masked, part) - m[:, half_of(part)]).astype(BF)
                    acc[:, part_at(b, part)] += dot(vt[:, units_at(u + PAD // UNIT, count)], p)

                far_sweep(plan, b, second, 0, 2, False)

    @pl.loop(0, chunks)
    def _(c):
        at = pl.ds(pl.multiple_of(c * rows, rows), rows)
        total_p = acc[head_width : head_width + 1, at]
        out = acc[:, at] / total_p
        o_ref[:, pl.ds(pl.multiple_of(c * rows + UNIT, UNIT), rows)] = out.astype(BF)
        of_ref[:, at] = out[: of_ref.shape[0]]
        lse_ref[:, at] = lse_ref[:, at] + jnp.log2(total_p)


def attend_forward(qkv, bounds, plan, table, head_width):
    chunks, packed_rows, rows = qkv.shape
    total = chunks * rows
    vm = pltpu.VMEM
    return pl.pallas_call(
        functools.partial(fwd_kernel, head_width=head_width),
        out_shape=(
            jax.ShapeDtypeStruct((SLOT, total + 2 * UNIT), BF),
            jax.ShapeDtypeStruct((40, total), F32),
            jax.ShapeDtypeStruct((1, total), F32),
        ),
        in_specs=[pl.BlockSpec(memory_space=pltpu.SMEM)] + [pl.BlockSpec()] * 3,
        scratch_shapes=[
            vm((3, DEPTH, total), BF),
            vm((total + 2 * PAD, DEPTH), BF),
            vm((SLOT, total + 2 * PAD), BF),
            vm((NEAR * UNIT, BLK), F32),
            vm((8, BLK), F32),
            vm((SLOT, total), F32),
        ],
        compiler_params=pltpu.CompilerParams(vmem_limit_bytes=62 * 2**20),
        name="attend_forward",
    )(plan, qkv, table, bounds)


def bwd_kernel(plan, qkv_ref, do_ref, of_ref, lse_ref, table_ref, bound_ref, dqkv_ref, dtab_ref,
               qaug, kn, kt, vn, dot_t, qn, don, tile, dq, band, ends, dv_acc, dk_acc, *, head_width):
    chunks, packed_rows, rows = qkv_ref.shape
    total = chunks * rows
    blocks = total // BLK
    span = table_ref.shape[1]
    table = pick_row(table_ref, lax.axis_index("head"))
    pick = spread_cols(packed_rows, 3, SLOT, head_width)
    scale = LOG2E / math.sqrt(head_width)
    back = 1.0 / math.sqrt(head_width)
    rest = DEPTH - 2 * SLOT
    bias_near(table, tile, False)
    for edge in (slice(0, PAD), slice(PAD + total, 2 * PAD + total)):
        for s in range(3):
            qaug[s, :, edge] = jnp.zeros((DEPTH, PAD), BF)
        dot_t[:, edge] = jnp.zeros((DEPTH, PAD), BF)
        qn[edge, :] = jnp.zeros((PAD, DEPTH), BF)
        don[edge, :] = jnp.zeros((PAD, DEPTH), BF)

    @pl.loop(0, chunks)
    def _(c):
        at = pl.ds(pl.multiple_of(c * rows, rows), rows)
        at_pad = pl.ds(pl.multiple_of(c * rows + PAD, UNIT), rows)
        parts = dot(pick, qkv_ref[c])
        q, k, v = parts[:SLOT], parts[SLOT : 2 * SLOT], parts[2 * SLOT :]
        qs = q * scale
        hi = qs.astype(BF)
        lo = (qs - hi.astype(F32)).astype(BF)
        lse = lse_ref[:, at]
        for s, shift in enumerate((table[:, :1] * LOG2E, 0.0, table[:, span - 1 :] * LOG2E)):
            qaug[s, :SLOT, at_pad] = hi
            qaug[s, SLOT : 2 * SLOT, at_pad] = lo
            qaug[s, 2 * SLOT :, at_pad] = three_rows(shift - lse, rest).astype(BF)
        one3 = (iota((rest, rows), 0) < 3).astype(F32)
        row48 = iota((SLOT, rows), 0)
        none = jnp.zeros((rest, rows), F32)
        empty = jnp.zeros((SLOT, rows), F32)
        kn[at, :] = jnp.concatenate([k, k, one3], axis=0).T.astype(BF)
        kt[:, at] = k.astype(BF)
        vn[at, :] = jnp.concatenate([v, empty, one3], axis=0).T.astype(BF)
        do = do_ref[c].astype(F32)
        centre = jnp.sum(do[: of_ref.shape[0]] * of_ref[:, at], axis=0, keepdims=True)
        dot_t[:SLOT, at_pad] = do_ref[c]
        dot_t[SLOT : 2 * SLOT, at_pad] = empty.astype(BF)
        dot_t[2 * SLOT :, at_pad] = three_rows(-centre, rest).astype(BF)
        qn[at_pad, :] = jnp.concatenate([q + (row48 == head_width).astype(F32), empty, none], axis=0).T.astype(BF)
        don[at_pad, :] = jnp.concatenate([do, empty, none], axis=0).T.astype(BF)

    dq[...] = jnp.zeros_like(dq)
    band[...] = jnp.zeros_like(band)
    ends[...] = jnp.zeros_like(ends)

    @pl.loop(0, blocks // GANG)
    def _(pair):
        width = NEAR * UNIT
        wide = width + (GANG - 1) * BLK
        blocks_now = [GANG * pair + i for i in range(GANG)]
        at_k = [units_at(PER * b, PER) for b in blocks_now]
        near = [units_at(PER * b - 1 + PAD // UNIT, NEAR) for b in blocks_now]
        x = [dot(kn[k, :], qaug[1, :, n]) + tile[...] for k, n in zip(at_k, near)]
        dp = [dot(vn[k, :], dot_t[:, n]) for k, n in zip(at_k, near)]
        p = [jnp.where(meets(b * BLK, BLK, bound_ref[:, n]), jnp.exp2(v), 0.0) for b, n, v in zip(blocks_now, near, x)]
        dsb = [(v * w).astype(BF) for v, w in zip(p, dp)]
        dv = [dot(v.astype(BF), don[n, :]) for n, v in zip(near, p)]
        dk = [dot(v, qn[n, :]) for n, v in zip(near, dsb)]
        part = [dot(kt[:, k], v) for k, v in zip(at_k, dsb)]
        for k, v, w in zip(at_k, dv, dk):
            dv_acc[k, :] = v
            dk_acc[k, :] = w
        gap = [jnp.zeros((SLOT, BLK), F32)]
        whole = [jnp.concatenate(gap * i + [v] + gap * (GANG - 1 - i), axis=1) for i, v in enumerate(part)]
        lines = [v.astype(F32) for v in dsb]
        dq[:, units_at(GANG * PER * pair - 1 + PAD // UNIT, wide // UNIT)] += functools.reduce(jnp.add, whole)
        band[...] += functools.reduce(jnp.add, lines)

    @pl.loop(0, blocks)
    def _(b):
        @pl.when(has_far(plan, b))
        def _():
            def far(u, count, side, masked, part):
                at_k = part_at(b, part)
                at_q = units_at(u + PAD // UNIT, count)
                p = jnp.exp2(dot(kn[at_k, :], qaug[side, :, at_q]))
                if masked:
                    first_key = b * BLK + (0 if part is None else part * BLK // 2)
                    p = jnp.where(meets(first_key, at_k.size, bound_ref[:, at_q]), p, 0.0)
                dsb = (p * dot(vn[at_k, :], dot_t[:, at_q])).astype(BF)
                dq[:, at_q] += dot(kt[:, at_k], dsb)
                dv_acc[at_k, :] += dot(p.astype(BF), don[at_q, :])
                dk = dot(dsb, qn[at_q, :])
                dk_acc[at_k, :] += dk
                ends[side // 2] += jnp.sum(dk.reshape(dk.shape[0] // 8, 8, DEPTH), axis=0)

            far_sweep(plan, b, far, 2, 0, True)

    def take(part, lanes):
        row, lane = iota((packed_rows, lanes), 0), iota((packed_rows, lanes), 1)
        return ((row - head_width * part == lane) & (lane < head_width)).astype(F32).astype(BF)

    @pl.loop(0, chunks)
    def _(c):
        at = pl.ds(pl.multiple_of(c * rows, rows), rows)
        at_pad = pl.ds(pl.multiple_of(c * rows + PAD, UNIT), rows)
        packed = dot(take(0, SLOT), (dq[:, at_pad] * back).astype(BF))
        packed += dot(take(1, DEPTH), (dk_acc[at, :] * back).astype(BF), NT)
        packed += dot(take(2, DEPTH), dv_acc[at, :].astype(BF), NT)
        dqkv_ref[c] = packed.astype(BF)

    flip = (iota((UNIT, UNIT), 0) + iota((UNIT, UNIT), 1) == UNIT - 1).astype(F32)
    half = span // 2
    lane = iota((8, span), 1)
    column = iota((8, DEPTH), 1) == head_width
    out = jnp.zeros((8, span), F32)
    far_sum = [jnp.where(column, ends[i], 0.0) for i in range(2)]
    for d in range(-PER, PER + 1):
        part = jnp.zeros((UNIT, UNIT), F32)
        for r in range(PER):
            c = r + d + 1
            if 0 <= c < NEAR:
                part = part + band[r * UNIT : (r + 1) * UNIT, c * UNIT : (c + 1) * UNIT]
        if abs(d) > 1:
            far_sum[0 if d > 0 else 1] += jnp.sum(part.reshape(UNIT // 8, 8, UNIT), axis=0)
            continue
        turned = lax.dot_general(flip, part, NN, precision=lax.Precision.HIGHEST, preferred_element_type=F32)
        wide = jnp.concatenate([turned, jnp.zeros_like(turned)], axis=1)
        skewed = pltpu.roll(wide, 0, 1, stride=1, stride_axis=0)
        line = jnp.sum(skewed.reshape(UNIT // 8, 8, 2 * UNIT), axis=0)
        offset = UNIT - 1 - d * UNIT - iota((span, 2 * UNIT), 1)
        hot = (jnp.clip(offset, -half, half - 1) + half == iota((span, 2 * UNIT), 0)).astype(F32)
        out += lax.dot_general(line, hot, NT, precision=lax.Precision.HIGHEST, preferred_element_type=F32)
    out += jnp.where(lane == 0, jnp.sum(far_sum[0], axis=1, keepdims=True), 0.0)
    out += jnp.where(lane == span - 1, jnp.sum(far_sum[1], axis=1, keepdims=True), 0.0)
    out = jnp.sum(out, axis=0, keepdims=True)
    dtab_ref[...] = out


def attend_backward(qkv, do, of, lse, bounds, plan, table, head_width):
    chunks, packed_rows, rows = qkv.shape
    total = chunks * rows
    padded = total + 2 * PAD
    span = table.shape[1]
    vm = pltpu.VMEM
    return pl.pallas_call(
        functools.partial(bwd_kernel, head_width=head_width),
        out_shape=(
            jax.ShapeDtypeStruct((chunks, packed_rows, rows), BF),
            jax.ShapeDtypeStruct((1, span), F32),
        ),
        in_specs=[pl.BlockSpec(memory_space=pltpu.SMEM)] + [pl.BlockSpec()] * 6,
        scratch_shapes=[
            vm((3, DEPTH, padded), BF),
            vm((total, DEPTH), BF),
            vm((SLOT, total), BF),
            vm((total, DEPTH), BF),
            vm((DEPTH, padded), BF),
            vm((padded, DEPTH), BF),
            vm((padded, DEPTH), BF),
            vm((BLK, NEAR * UNIT), F32),
            vm((SLOT, padded), F32),
            vm((BLK, NEAR * UNIT), F32),
            vm((2, 8, DEPTH), F32),
            vm((total, DEPTH), F32),
            vm((total, DEPTH), F32),
        ],
        compiler_params=pltpu.CompilerParams(vmem_limit_bytes=62 * 2**20),
        name="attend_backward",
    )(plan, qkv, do, of, lse, table, bounds)

VEC = types.SimpleNamespace(
    first_gain=0, first_shift=1, first_up_bias=2, first_down_bias=3, mix_gain=4, mix_shift=5, mix_output_bias=6, filter_gain=7,
    filter_shift=8, pointwise_in_bias=9, batch_gain=10, batch_shift=11, pointwise_out_bias=12, second_gain=13, second_shift=14,
    second_up_bias=15, second_down_bias=16, final_gain=17, final_shift=18,
)
VEC_ROWS = 24
EPSILON = 1e-05
HALO = 64
TILE = 128
PIECE = 256


def col(cols_ref, i, size):
    return cols_ref[:size, i : i + 1]


def eye(n):
    return (iota((n, n), 0) == iota((n, n), 1)).astype(F32).astype(BF)


def flipped(mat):
    return dot(eye(mat.shape[1]), mat, NT).astype(BF)


def exact(a, b, dims=NN):
    return lax.dot_general(a, b, dims, precision=lax.Precision.HIGHEST, preferred_element_type=F32)


def folded(values):
    part = values[:, :TILE]
    for at in range(TILE, values.shape[1], TILE):
        part = part + values[:, at : at + TILE]
    return part


def row_sums(values):
    return exact(jnp.ones((8, TILE), F32), values, NT)


def norm(x):
    m = jnp.mean(x, axis=0, keepdims=True)
    c = x - m
    inv = lax.rsqrt(jnp.mean(c * c, axis=0, keepdims=True) + EPSILON)
    return c * inv, inv


def norm_back(e, n, inv, gain):
    ea = e * gain
    return inv * (ea - jnp.mean(ea, axis=0, keepdims=True) - n * jnp.mean(ea * n, axis=0, keepdims=True))


def sigmoid(v):
    return 0.5 + 0.5 * jnp.tanh(0.5 * v)


def ones_row(rows, lanes):
    return (iota((rows, lanes), 0) == 0).astype(F32).astype(BF)


def open_rows(frames_ref, up_ref, down_ref, mix_ref, x1_ref, h2_ref, qkv_ref, cols_ref, packed_rows, ship):
    width, rows = frames_ref.shape
    hidden = up_ref.shape[1]
    heads = qkv_ref.shape[0]
    up_t = flipped(up_ref[...])
    mix_t = dot(spread_cols(mix_ref.shape[1], heads, packed_rows, mix_ref.shape[1] // heads), mix_ref[...], NT).astype(BF)

    @pl.loop(0, rows // PIECE)
    def _(c):
        at = pl.ds(pl.multiple_of(c * PIECE, PIECE), PIECE)
        x0 = frames_ref[:, at].astype(F32)
        n, _ = norm(x0)
        h1 = (n * col(cols_ref, VEC.first_gain, width) + col(cols_ref, VEC.first_shift, width)).astype(BF)
        a1 = dot(up_t, h1) + col(cols_ref, VEC.first_up_bias, hidden)
        s1 = (a1 * sigmoid(a1)).astype(BF)
        x1 = x0 + 0.5 * (dot(down_ref[...], s1) + col(cols_ref, VEC.first_down_bias, width))
        x1_ref[:, at] = x1
        n, _ = norm(x1)
        h2 = (n * col(cols_ref, VEC.mix_gain, width) + col(cols_ref, VEC.mix_shift, width)).astype(BF)
        h2_ref[:, at] = h2
        qkv = dot(mix_t, h2).astype(BF)
        for h in range(heads):
            qkv_ref[h, :, at] = qkv[h * packed_rows : (h + 1) * packed_rows]
        ship(c)


def open_segments(len_ref, bound_ref, plan_ref, ext_ref, line):
    rows = ext_ref.shape[1] - TILE
    group = bound_ref.shape[1] - 2 * PAD
    slots = len_ref.shape[1]
    lengths = jnp.broadcast_to(len_ref[...].astype(F32), (8, slots))
    row, column = iota((slots, slots), 0), iota((slots, slots), 1)
    ends = exact((column <= row).astype(F32), lengths, NT)[:, :1].astype(jnp.int32)
    own_len = exact((column == row).astype(F32), lengths, NT)[:, :1].astype(jnp.int32)
    ends_row = exact(lengths, (row <= column).astype(F32))[:1].astype(jnp.int32)
    plan_ref[...] = block_plan(ends, ends_row, group)
    line[...] = jnp.full_like(line, -1)
    for edge in (slice(0, PAD), slice(PAD + group, 2 * PAD + group)):
        bound_ref[:, edge] = jnp.where(iota((2, PAD), 0) == 0, 1 << 20, -1)

    @pl.loop(0, group // 512)
    def _(c):
        at = pl.multiple_of(c * 512, 512)
        seg, first, stop = segment_rows(ends, own_len, iota((1, 512), 1) + at, group)
        line[:, pl.ds(at + TILE, 512)] = seg
        bound_ref[0:1, pl.ds(at + PAD, 512)] = first
        bound_ref[1:2, pl.ds(at + PAD, 512)] = stop

    first = pl.multiple_of(lax.axis_index("head") * rows, TILE)
    ext_ref[:, :rows] = line[:, pl.ds(first + TILE, rows)]
    left = line[:, pl.ds(first, TILE)]
    right = line[:, pl.ds(first + TILE + rows, TILE)]
    ext_ref[:, rows:] = jnp.where(iota((1, TILE), 1) < HALO, right, left)


def conv_masks(mask_ref, ext_ref):
    seg = jnp.broadcast_to(ext_ref[...], (8, ext_ref.shape[1]))
    lanes = seg.shape[1]
    reach = mask_ref.shape[0] // 2
    for i in range(mask_ref.shape[0]):
        mask_ref[i] = (pltpu.roll(seg, (reach - i) % lanes, 1) == seg).astype(F32)


def filter_kernel(x1_ref, x1l_ref, x1r_ref, o_ref, cols_ref, ext_ref, out_ref, pw_ref, taps_ref,
                  x2_ref, oc_ref, u_ref, y_ref, stat_ref, wide, mask, live_ref, h3s, n_ref, inv_ref, value_ref, gate_ref, *, head_width, slot_count, arrive):
    width, rows = x1_ref.shape
    lanes = rows + TILE
    heads = o_ref.shape[0]
    taps = taps_ref.shape[0]
    out_t = flipped(out_ref[...])
    pw_t = flipped(pw_ref[...])
    gather = spread_cols(width, heads, SLOT, head_width)
    seg = ext_ref[...]
    live = (seg >= 0) & (seg < slot_count)
    live_ref[...] = live.astype(F32)
    conv_masks(mask, ext_ref)
    wide_taps = taps_ref[...].astype(F32).T
    arrive()

    near = iota((1, TILE), 1) < HALO

    def extended(own, left, right):
        edge = jnp.where(near, right.astype(F32), left.astype(F32)).astype(own.dtype)
        return jnp.concatenate([own, edge], axis=1)

    x1 = extended(x1_ref[...], x1l_ref[...], x1r_ref[...])
    o = jnp.concatenate(
        [extended(o_ref[h, :, TILE : TILE + rows], o_ref[h, :, :TILE], o_ref[h, :, TILE + rows :]) for h in range(heads)], axis=0)
    oc = dot(gather, o, TN).astype(BF)
    x2 = x1 + (dot(out_t, oc) + col(cols_ref, VEC.mix_output_bias, width))
    n, inv = norm(x2)
    h3 = (n * col(cols_ref, VEC.filter_gain, width) + col(cols_ref, VEC.filter_shift, width)).astype(BF)
    g = dot(pw_t, h3) + col(cols_ref, VEC.pointwise_in_bias, 2 * width)
    gate = sigmoid(g[width:])
    u = jnp.where(live_ref[...] > 0.5, g[:width] * gate, 0.0).astype(BF)
    n_ref[...] = n[:, :rows]
    inv_ref[...] = inv[:, :rows]
    h3s[:width, :] = h3[:, :rows]
    value_ref[...] = g[:width, :rows]
    gate_ref[...] = gate[:, :rows]
    oc_ref[:width, :] = oc[:, :rows]
    x2_ref[...] = x2
    u_ref[...] = u
    wide[...] = u.astype(F32)

    own = (live & (iota((1, lanes), 1) < rows)).astype(F32)
    count = jnp.sum(own, axis=1, keepdims=True)
    safe = jnp.maximum(count, 1.0)
    for r in range(width // 8):
        sl = slice(8 * r, 8 * r + 8)
        u8 = wide[sl, :]
        acc = jnp.zeros((8, lanes), F32)
        for k in range(taps):
            moved = pltpu.roll(u8, (taps // 2 - k) % lanes, 1)
            acc = acc + wide_taps[sl, k : k + 1] * (moved * mask[k])
        y_ref[sl, :] = acc
    y = y_ref[...]
    part = folded(y * own)
    mean = exact(part, jnp.ones((TILE, TILE), F32)) / safe
    dev = (y - jnp.concatenate([mean] * (lanes // TILE), axis=1)) * own
    stat_ref[...] = two_rows(row_sums(part)[:1] / safe, row_sums(folded(dev * dev))[:1], count)


def two_rows(a, b, extra):
    rest = a.shape[1] - TILE
    tail = pad_lanes(jnp.concatenate([a[:, TILE:], b[:, TILE:]], axis=0))
    spot = (iota((2, TILE), 0) == 0) & (iota((2, TILE), 1) == rest)
    return jnp.concatenate([a[:, :TILE], b[:, :TILE], jnp.where(spot, extra, tail)], axis=0)


def all_rows(ref, width):
    rest = width - TILE
    values = ref[...]
    a = jnp.concatenate([values[:, 0, :], values[:, 2, :rest]], axis=1)
    b = jnp.concatenate([values[:, 1, :], values[:, 3, :rest]], axis=1)
    return a, b, values[:, 2, rest : rest + 1]


def total_stats(stats_ref, width):
    mean_of, spread_of, n = all_rows(stats_ref, width)
    count = jnp.sum(n, axis=0, keepdims=True)
    mean = jnp.sum(n * mean_of, axis=0, keepdims=True) / count
    gap = mean_of - mean
    spread = jnp.sum(spread_of + n * gap * gap, axis=0, keepdims=True)
    inv = lax.rsqrt(spread / count + EPSILON)
    table = jnp.concatenate([mean, inv, jnp.broadcast_to(count, (1, width)), jnp.zeros((5, width), F32)], axis=0).T
    return table[:, 0:1], table[:, 1:2], table[:, 2:3]


def second_kernel(x2_ref, y_ref, stats_ref, cot_ref, cotl_ref, cotr_ref, cols_ref, pwo_ref, up_ref, down_ref,
                  out_ref, dx3_ref, e_ref, sums_ref, pack_ref, small_ref,
                  h4s, das, s4s, dfs, ws, dcs, *, arrive, leave):
    width, rows = out_ref.shape
    hidden = up_ref.shape[1]
    pwo_t = flipped(pwo_ref[...])
    up_t = flipped(up_ref[...])
    down = flipped(down_ref[...])
    arrive()
    mean, inv_b, _ = total_stats(stats_ref, width)
    bgain = col(cols_ref, VEC.batch_gain, width)

    near = iota((1, TILE), 1) < HALO
    edge = jnp.where(near, cotr_ref[...].astype(F32), cotl_ref[...].astype(F32))
    cot = jnp.concatenate([cot_ref[...].astype(F32), edge], axis=1)
    zh = (y_ref[...] - mean) * inv_b
    z = zh * bgain + col(cols_ref, VEC.batch_shift, width)
    sig_z = sigmoid(z)
    w = (z * sig_z).astype(BF)
    x3 = x2_ref[...] + (dot(pwo_t, w) + col(cols_ref, VEC.pointwise_out_bias, width))
    n4, inv4 = norm(x3)
    h4 = (n4 * col(cols_ref, VEC.second_gain, width) + col(cols_ref, VEC.second_shift, width)).astype(BF)
    a4 = dot(up_t, h4) + col(cols_ref, VEC.second_up_bias, hidden)
    sig = sigmoid(a4)
    s4 = (a4 * sig).astype(BF)
    x4 = x3 + 0.5 * (dot(down_ref[...], s4) + col(cols_ref, VEC.second_down_bias, width))
    nf, invf = norm(x4)
    fgain = col(cols_ref, VEC.final_gain, width)
    dx4 = norm_back(cot, nf, invf, fgain)
    df = (0.5 * dx4).astype(BF)
    da = (dot(down, df) * (sig * (1.0 + a4 * (1.0 - sig)))).astype(BF)
    dh = dot(up_ref[...], da)
    dx3 = dx4 + norm_back(dh, n4, inv4, col(cols_ref, VEC.second_gain, width))
    dc = dx3.astype(BF)
    dz = dot(pwo_ref[...], dc) * (sig_z * (1.0 + z * (1.0 - sig_z)))
    e = dz * bgain
    e_ref[...] = e
    sums_ref[...] = two_rows(row_sums(folded(e[:, :rows]))[:1], row_sums(folded((e * zh)[:, :rows]))[:1], 0.0)
    leave()

    out_ref[...] = (nf * fgain + col(cols_ref, VEC.final_shift, width))[:, :rows].astype(BF)
    dx3_ref[...] = dx3[:, :rows]
    h4s[...] = h4[:, :rows]
    das[...] = da[:, :rows]
    s4s[:hidden, :] = s4[:, :rows]
    dfs[...] = df[:, :rows]
    ws[:width, :] = w[:, :rows]
    dcs[...] = dc[:, :rows]
    totals = [row_sums(folded(v[:, :rows]))[:1] for v in (dh * n4, dh, cot * nf, cot, dz * zh, dz)]
    s4s[hidden:, :] = ones_row(16, rows)
    ws[width:, :] = ones_row(16, rows)
    up_grad = dot(h4s[...], das[...], NT)
    up_bias = dot(ones_row(16, rows), das[...], NT)
    down_grad = dot(dfs[...], s4s[...], NT)
    pw_grad = dot(ws[...], dcs[...], NT)
    down_bias = exact(jnp.ones((8, rows), F32), dfs[...].astype(F32), NT)
    put_ff(pack_ref, up_grad, down_grad, 0)
    tall = 9 * width
    pack_ref[tall : tall + width, :] = pw_grad[:width, :TILE].astype(BF)
    pack_ref[tall + width : tall + 2 * width, :] = pad_lanes(pw_grad[:width, TILE:]).astype(BF)
    small_ref[...] = stack_rows(
        [totals[0], totals[1], up_bias[:1], down_bias[:1], totals[2], totals[3], totals[4], totals[5], pw_grad[width : width + 1]],
        small_ref.shape)


def pad_lanes(mat, lanes=TILE):
    if mat.shape[1] == lanes:
        return mat
    return jnp.concatenate([mat, jnp.zeros((mat.shape[0], lanes - mat.shape[1]), mat.dtype)], axis=1)


def stack_rows(rows, shape):
    parts = [pad_lanes(r, shape[1]) for r in rows]
    parts.append(jnp.zeros((shape[0] - len(rows), shape[1]), F32))
    return jnp.concatenate(parts, axis=0)


def put_ff(pack_ref, up_grad, down_grad_t, at):
    width, hidden = up_grad.shape
    whole = hidden // TILE
    for i in range(whole):
        pack_ref[at + i * width : at + (i + 1) * width, :] = up_grad[:, i * TILE : (i + 1) * TILE].astype(BF)
        j = whole + i
        pack_ref[at + j * width : at + (j + 1) * width, :] = down_grad_t[:, i * TILE : (i + 1) * TILE].astype(BF)
    rest = jnp.concatenate([up_grad[:, whole * TILE : hidden], down_grad_t[:, whole * TILE : hidden]], axis=1)
    pack_ref[at + 2 * whole * width : at + (2 * whole + 1) * width, :] = rest.astype(BF)


def unfilter_kernel(e_ref, y_ref, stats_ref, sums_ref, u_ref, dx3_ref, ocs, cols_ref, ext_ref, pw_ref, taps_ref,
                    out_ref, dx2_ref, do_ref, pack_ref, small_ref, tapg_ref,
                    dyw, du_s, mask, prod, h3s, dgs, dms, gains, live_ref, n_ref, inv_ref, value_ref, gate_ref, *, head_width, ship, arrive):
    width, rows = dx3_ref.shape
    lanes = rows + TILE
    heads = do_ref.shape[0]
    taps = taps_ref.shape[0]
    tap_cols = taps_ref[...].astype(F32).T
    out_w = dot(spread_cols(width, heads, SLOT, head_width), out_ref[...]).astype(BF)
    gains[...] = jnp.zeros_like(gains)
    fgain = col(cols_ref, VEC.filter_gain, width)
    mean, inv_b, count = total_stats(stats_ref, width)
    arrive()
    one_of, two_of, _ = all_rows(sums_ref, width)
    sums = jnp.concatenate([jnp.sum(one_of, axis=0, keepdims=True), jnp.sum(two_of, axis=0, keepdims=True), jnp.zeros((6, width), F32)], axis=0).T
    s1, s2 = sums[:, 0:1], sums[:, 1:2]
    seg = ext_ref[...]
    live = live_ref[...]
    zh = (y_ref[...] - mean) * inv_b
    dy = inv_b * (e_ref[...] - live * ((s1 + zh * s2) / count))
    dyw[...] = jnp.where(seg >= 0, dy, 0.0).astype(BF).astype(F32)

    for r in range(width // 8):
        sl = slice(8 * r, 8 * r + 8)
        dy8 = dyw[sl, :]
        u8 = u_ref[16 * (r // 2) : 16 * (r // 2) + 16, :rows].astype(F32)[8 * (r % 2) : 8 * (r % 2) + 8]
        acc = jnp.zeros((8, rows), F32)
        for k in range(taps):
            moved = pltpu.roll(dy8, (k - taps // 2) % lanes, 1)[:, :rows] * mask[taps - k][:, :rows]
            acc = acc + tap_cols[sl, k : k + 1] * moved
            hit = moved * u8
            prod[k, sl, :] = folded(hit)
        du_s[sl, :] = acc

    @pl.loop(0, rows // PIECE)
    def _(c):
        at = pl.ds(pl.multiple_of(c * PIECE, PIECE), PIECE)
        n, inv = n_ref[:, at], inv_ref[:, at]
        gate = gate_ref[:, at]
        t = live_ref[:, at] * du_s[:, at] * gate
        dg = jnp.concatenate([t, t * value_ref[:, at] * (1.0 - gate)], axis=0).astype(BF)
        dh = dot(pw_ref[...], dg)
        dx2 = dx3_ref[:, at] + norm_back(dh, n, inv, fgain)
        dx2_ref[:, at] = dx2
        dm = dx2.astype(BF)
        do = dot(out_w, dm).astype(BF)
        for h in range(heads):
            do_ref[h, :, at] = do[h * SLOT : (h + 1) * SLOT]
        ship(c)
        dgs[:, at] = dg
        dms[:, at] = dm
        for i, v in enumerate((dh * n, dh)):
            gains[i] += folded(v)

    whole = prod[...].reshape(taps * width, TILE)
    hi = whole.astype(BF)
    lo = (whole - hi.astype(F32)).astype(BF)
    ones = jnp.ones((8, TILE), BF)
    lines = dot(ones, hi, NT) + dot(ones, lo, NT)
    for k in range(taps):
        tapg_ref[k : k + 1, :] = lines[:1, k * width : (k + 1) * width]

    h3s[width:, :] = ones_row(16, rows)
    ocs[width:, :] = ones_row(16, rows)
    pw_grad = dot(h3s[...], dgs[...], NT)
    out_grad = dot(ocs[...], dms[...], NT)
    at = 0
    for lo in range(0, 2 * width, TILE):
        pack_ref[at : at + width, :] = pad_lanes(pw_grad[:width, lo : min(lo + TILE, 2 * width)]).astype(BF)
        at += width
    for lo in range(0, width, TILE):
        pack_ref[at : at + width, :] = pad_lanes(out_grad[:width, lo : min(lo + TILE, width)]).astype(BF)
        at += width
    small_ref[...] = stack_rows(
        [row_sums(gains[0])[:1], row_sums(gains[1])[:1], pw_grad[width : width + 1], out_grad[width : width + 1]], small_ref.shape)


def close_kernel(frames_ref, x1_ref, h2_ref, dx2_ref, dqkv_ref, dtab_ref, cols_ref, up_ref, down_ref, mix_ref,
                 grad_ref, pack_ref, h1s, das, s1s, dfs, dqs, gains, up_part, down_part, mix_part, *, arrive, between, mixed):
    width, rows = frames_ref.shape
    most = slice(0, rows - PIECE)
    hidden = up_ref.shape[1]
    heads, packed_rows, _ = dqkv_ref.shape
    up_t = flipped(up_ref[...])
    down = flipped(down_ref[...])
    hot = spread_cols(mix_ref.shape[1], heads, packed_rows, mix_ref.shape[1] // heads)
    mix_w = dot(mix_ref[...], hot, NT).astype(BF)
    gains[...] = jnp.zeros_like(gains)
    mgain = col(cols_ref, VEC.mix_gain, width)
    fgain = col(cols_ref, VEC.first_gain, width)

    @pl.loop(0, rows // PIECE)
    def _(c):
        arrive(c)
        at = pl.ds(pl.multiple_of(c * PIECE, PIECE), PIECE)
        dq = jnp.concatenate([dqkv_ref[h, :, at] for h in range(heads)], axis=0)
        dqs[:, at] = dq
        dh2 = dot(mix_w, dq)
        n2, inv2 = norm(x1_ref[:, at])
        dx1 = dx2_ref[:, at] + norm_back(dh2, n2, inv2, mgain)
        x0 = frames_ref[:, at].astype(F32)
        n1, inv1 = norm(x0)
        h1 = (n1 * fgain + col(cols_ref, VEC.first_shift, width)).astype(BF)
        a1 = dot(up_t, h1) + col(cols_ref, VEC.first_up_bias, hidden)
        sig = sigmoid(a1)
        s1s[:, at] = (a1 * sig).astype(BF)
        df = (0.5 * dx1).astype(BF)
        da = (dot(down, df) * (sig * (1.0 + a1 * (1.0 - sig)))).astype(BF)
        dh1 = dot(up_ref[...], da)
        grad_ref[:, at] = dx1 + norm_back(dh1, n1, inv1, fgain)
        h1s[:, at] = h1
        das[:, at] = da
        dfs[:, at] = df
        for i, v in enumerate((dh1 * n1, dh1, dh2 * n2, dh2)):
            gains[i] += folded(v)
        between(c)

        @pl.when(c == rows // PIECE - 2)
        def _():
            up_part[...] = dot(h1s[:, most], das[:, most], NT)
            down_part[...] = dot(dfs[:, most], s1s[:, most], NT)
            mix_part[...] = dot(h2_ref[:, most], dqs[:, most], NT)

    rest = slice(rows - PIECE, rows)
    mix_grad = dot((mix_part[...] + dot(h2_ref[:, rest], dqs[:, rest], NT)).astype(BF), hot)
    at = 0
    for lo in range(0, mix_grad.shape[1], TILE):
        pack_ref[at : at + width, :] = pad_lanes(mix_grad[:, lo : min(lo + TILE, mix_grad.shape[1])]).astype(BF)
        at += width
    mixed()
    up_grad = up_part[...] + dot(h1s[:, rest], das[:, rest], NT)
    up_bias = dot(ones_row(16, rows), das[...], NT)
    down_grad = down_part[...] + dot(dfs[:, rest], s1s[:, rest], NT)
    down_bias = exact(jnp.ones((8, rows), F32), dfs[...].astype(F32), NT)
    put_ff(pack_ref, up_grad, down_grad, at)
    at += (2 * (hidden // TILE) + 1) * width
    totals = [row_sums(gains[i])[:1] for i in range(4)]
    small = stack_rows([totals[0], totals[1], up_bias[:1], down_bias[:1], totals[2], totals[3]], (16, 5 * TILE))
    at = put_small(pack_ref, small, at)
    span = dtab_ref.shape[1]
    table = jnp.where(iota((16, span), 0) == lax.axis_index("head"), dtab_ref[...], 0.0)
    pack_ref[at : at + 16, :] = table.astype(BF)
    if at + 16 < pack_ref.shape[0]:
        pack_ref[at + 16 :, :] = jnp.zeros((pack_ref.shape[0] - at - 16, TILE), BF)


def put_small(pack_ref, small, at):
    for lo in range(0, small.shape[1], TILE):
        pack_ref[at : at + small.shape[0], :] = small[:, lo : lo + TILE].astype(BF)
        at += small.shape[0]
    return at


def put_taps(pack_ref, tapg, at):
    taps = tapg.shape[0]
    pack_ref[at : at + taps, :] = tapg[:, :TILE].astype(BF)
    pack_ref[at + taps : at + 2 * taps, :] = pad_lanes(tapg[:, TILE:]).astype(BF)
    return at + 2 * taps


def unpack_kernel(pack_ref, out_ref, grad_ref, *refs, layout):
    refs[0][...] = out_ref[...]
    refs[1][...] = grad_ref[...]
    out_refs = refs[2:]
    given = Weights(*out_refs)

    def wide(at, rows, lanes):
        parts = [pack_ref[at + i * rows : at + (i + 1) * rows, :].astype(F32) for i in range(-(-lanes // TILE))]
        return jnp.concatenate(parts, axis=1)[:, :lanes]

    for at, up_ref, down_ref in ((layout.first, given.first_up, given.first_down), (layout.second, given.second_up, given.second_down)):
        width, hidden = up_ref.shape
        whole = hidden // TILE
        half = hidden - whole * TILE
        piece = lambda i: pack_ref[at + i * width : at + (i + 1) * width, :].astype(F32)
        rest = piece(2 * whole)
        up_ref[...] = jnp.concatenate([piece(i) for i in range(whole)] + [rest[:, :half]], axis=1)
        down_ref[...] = jnp.concatenate([piece(whole + i) for i in range(whole)] + [rest[:, half:]], axis=1)
    for ref, at in ((given.mix_inputs, layout.mix_inputs), (given.pointwise_in, layout.pointwise_in), (given.mix_output, layout.mix_output),
                    (given.pointwise_out, layout.pointwise_out), (given.depthwise_taps, layout.taps)):
        ref[...] = wide(at, *ref.shape)
    given.position_bias[...] = pack_ref[layout.table : layout.table + 16, :].astype(F32)[: given.position_bias.shape[0]]
    late = wide(layout.small_late, 16, 5 * TILE)
    early = wide(layout.small, 32, 5 * TILE)
    late_rows = (
        given.first_gain, given.first_shift, given.first_up_bias, given.first_down_bias, given.mix_gain, given.mix_shift,
    )
    second_rows = (
        given.second_gain, given.second_shift, given.second_up_bias, given.second_down_bias, given.final_gain, given.final_shift,
        given.batch_gain, given.batch_shift, given.pointwise_out_bias,
    )
    filter_rows = (given.filter_gain, given.filter_shift, given.pointwise_in_bias, given.mix_output_bias)
    for small, first, refs in ((late, 0, late_rows), (early, 0, second_rows), (early, 16, filter_rows)):
        for row, ref in enumerate(refs, first):
            ref[...] = small[row : row + 1, : ref.shape[0]].reshape(ref.shape)


@dataclasses.dataclass
class Weights:
    first_gain: object
    first_shift: object
    first_up: object
    first_up_bias: object
    first_down: object
    first_down_bias: object
    mix_gain: object
    mix_shift: object
    mix_inputs: object
    position_bias: object
    mix_output: object
    mix_output_bias: object
    filter_gain: object
    filter_shift: object
    pointwise_in: object
    pointwise_in_bias: object
    depthwise_taps: object
    batch_gain: object
    batch_shift: object
    pointwise_out: object
    pointwise_out_bias: object
    second_gain: object
    second_shift: object
    second_up: object
    second_up_bias: object
    second_down: object
    second_down_bias: object
    final_gain: object
    final_shift: object


def pack_layout(width, hidden, mix_width, taps, devices):
    ff = (2 * (hidden // TILE) + 1) * width
    chunks = lambda lanes: -(-lanes // TILE) * width
    unit = 16 * devices
    whole = lambda rows: -(-rows // unit) * unit
    at = types.SimpleNamespace(second=0, pointwise_out=ff)
    at.pointwise_in = ff + chunks(width)
    at.mix_output = at.pointwise_in + chunks(2 * width)
    at.taps = at.mix_output + chunks(width)
    at.small = at.taps + 2 * taps
    at.late = at.mix_inputs = whole(at.small + 32 * 5)
    at.last = at.late + chunks(mix_width) // unit * unit
    at.first = at.mix_inputs + chunks(mix_width)
    at.small_late = at.first + ff
    at.table = at.small_late + 16 * 5
    at.rows = at.late + whole(at.table + 16 - at.late)
    return at


MESH = pl.DeviceIdType.MESH


def meet(peers):
    barrier = pltpu.get_barrier_semaphore()
    for peer in peers:
        pl.semaphore_signal(barrier, inc=1, device_id=peer, device_id_type=MESH)
    pl.semaphore_wait(barrier, len(peers))


def head_peers(n):
    me = lax.axis_index("head")
    return me, [{"head": lax.rem(me + s, n)} for s in range(1, n)], [lax.rem(me + s, n) for s in range(1, n)]


def opening_kernel(frames_ref, len_ref, up_ref, down_ref, mix_ref, *refs, packed_rows, n):
    count = len(VEC.__dict__)
    vec_refs, refs = refs[:count], refs[count:]
    (cot_ref, x1_ref, h2_ref, cols_ref, bound_ref, plan_ref, ext_ref, all_ref, x1l_ref, x1r_ref, cotl_ref, cotr_ref,
     qkv, line, send, recv, local, hsend, hrecv) = refs
    me, peers, ids = head_peers(n)
    rows = cot_ref.shape[1]
    barrier = pltpu.get_barrier_semaphore()
    for peer in peers:
        pl.semaphore_signal(barrier, inc=1, device_id=peer, device_id_type=MESH)
    vecs = [ref[...].astype(F32).reshape(1, ref.shape[0]) for ref in vec_refs]
    cols_ref[...] = stack_rows(vecs, (VEC_ROWS, up_ref.shape[1])).T
    pl.semaphore_wait(barrier, len(peers))

    def piece(c, s):
        at = pl.ds(pl.multiple_of(c * PIECE, PIECE), PIECE)
        return pltpu.make_async_remote_copy(src_ref=qkv.at[ids[s], :, at], dst_ref=all_ref.at[me, :, at], send_sem=send.at[c, s],
                                            recv_sem=recv.at[c, s], device_id=peers[s], device_id_type=MESH)

    def ship(c):
        for s in range(n - 1):
            piece(c, s).start()

    open_rows(frames_ref, up_ref, down_ref, mix_ref, x1_ref, h2_ref, qkv, cols_ref, packed_rows, ship)
    own = pltpu.make_async_copy(qkv.at[me], all_ref.at[me], local)
    own.start()

    def edge(i, src, dst, head):
        return pltpu.make_async_remote_copy(src_ref=src, dst_ref=dst, send_sem=hsend.at[i], recv_sem=hrecv.at[i],
                                            device_id={"head": head}, device_id_type=MESH)

    up = lax.rem(me + 1, n)
    down = lax.rem(me + n - 1, n)
    last, start = pl.ds(rows - TILE, TILE), pl.ds(0, TILE)
    to_right = [edge(0, x1_ref.at[:, last], x1l_ref, up), edge(1, cot_ref.at[:, last], cotl_ref, up)]
    to_left = [edge(2, x1_ref.at[:, start], x1r_ref, down), edge(3, cot_ref.at[:, start], cotr_ref, down)]

    @pl.when(me < n - 1)
    def _():
        for c in to_right:
            c.start()

    @pl.when(me > 0)
    def _():
        for c in to_left:
            c.start()

    open_segments(len_ref, bound_ref, plan_ref, ext_ref, line)
    own.wait()

    @pl.loop(0, rows // PIECE)
    def _(c):
        for s in range(n - 1):
            piece(c, s).wait()

    @pl.when(me < n - 1)
    def _():
        for c in to_right:
            c.wait_send()
        for c in to_left:
            c.wait_recv()

    @pl.when(me > 0)
    def _():
        for c in to_left:
            c.wait_send()
        for c in to_right:
            c.wait_recv()


def everyone(n_tm, n_head):
    n = n_tm * n_head
    me = lax.axis_index("tm") * n_head + lax.axis_index("head")

    def place(s):
        peer = lax.rem(me + s, n)
        return {"tm": peer // n_head, "head": lax.rem(peer, n_head)}

    return me, n, place


def tell(src_ref, all_ref, send, recv, n_tm, n_head):
    me, n, place = everyone(n_tm, n_head)

    def copy(s):
        return pltpu.make_async_remote_copy(src_ref=src_ref, dst_ref=all_ref.at[me], send_sem=send.at[s], recv_sem=recv.at[s],
                                            device_id=place(s), device_id_type=MESH)

    def start():
        pl.loop(1, n)(lambda s: copy(s).start())
        all_ref[me] = src_ref[...]

    def end():
        pl.loop(1, n)(lambda s: copy(s).wait())

    return start, end


def load_all(sources, targets, sems):
    copies = [pltpu.make_async_copy(src, dst, sems.at[i]) for i, (src, dst) in enumerate(zip(sources, targets))]
    for copy in copies:
        copy.start()
    return copies


def middle_kernel(*refs, n_tm, n_head, head_width, slot_count, layout):
    o_ref, sources, refs = refs[0], refs[1:15], refs[15:]
    (out_ref, dx2_ref, do_all, pack_ref), refs = refs[:4], refs[4:]
    loaded, refs = refs[:14], refs[14:]
    (x1_ref, x1l_ref, x1r_ref, cot_ref, cotl_ref, cotr_ref, cols_ref, ext_ref, mixo_ref, pwi_ref, taps_ref, pwo_ref, up_ref,
     down_ref) = loaded
    (o_own, x2, oc, u, y, stat, stats, dx3, e, sums, all_sums, do, wide, mask, live,
     h4s, das, s4s, dfs, ws, dcs, dyw, du, prod, h3s, dgs, dms, gains2, smalld, smalle, tapg,
     n3, inv3, value3, gate3), refs = refs[:35], refs[35:]
    (load_sems, send_o, recv_o, local_o, send_a, recv_a, send_b, recv_b, send_d, recv_d, local_d) = refs
    me, peers, ids = head_peers(n_head)
    _, n, place = everyone(n_tm, n_head)
    barrier = pltpu.get_barrier_semaphore()
    rows = x1_ref.shape[1]

    @pl.loop(1, n)
    def _(s):
        pl.semaphore_signal(barrier, inc=1, device_id=place(s), device_id_type=MESH)

    loads = load_all(sources, loaded, load_sems)
    pl.semaphore_wait(barrier, n - 1)

    def part(p):
        return o_ref.at[:, pl.ds(pl.multiple_of(p * rows, TILE), rows + 2 * TILE)]

    copies = [
        pltpu.make_async_remote_copy(src_ref=part(p), dst_ref=o_own.at[me], send_sem=send_o.at[s], recv_sem=recv_o.at[s],
                                     device_id=peer, device_id_type=MESH)
        for s, (peer, p) in enumerate(zip(peers, ids))
    ]
    for copy in copies:
        copy.start()
    own = pltpu.make_async_copy(part(me), o_own.at[me], local_o)
    own.start()
    for load in loads:
        load.wait()

    def arrive():
        own.wait()
        for copy in copies:
            copy.wait()

    filter_kernel(x1_ref, x1l_ref, x1r_ref, o_own, cols_ref, ext_ref, mixo_ref, pwi_ref, taps_ref, x2, oc, u, y, stat, wide, mask, live,
                  h3s, n3, inv3, value3, gate3, head_width=head_width, slot_count=slot_count, arrive=arrive)
    stats_out, stats_in = tell(stat, stats, send_a, recv_a, n_tm, n_head)
    sums_out, sums_in = tell(sums, all_sums, send_b, recv_b, n_tm, n_head)
    stats_out()
    second_kernel(x2, y, stats, cot_ref, cotl_ref, cotr_ref, cols_ref, pwo_ref, up_ref, down_ref,
                  out_ref, dx3, e, sums, pack_ref, smalld, h4s, das, s4s, dfs, ws, dcs, arrive=stats_in, leave=sums_out)

    def piece(c, s):
        at = pl.ds(pl.multiple_of(c * PIECE, PIECE), PIECE)
        return pltpu.make_async_remote_copy(src_ref=do.at[ids[s], :, at], dst_ref=do_all.at[me, :, at], send_sem=send_d.at[c, s],
                                            recv_sem=recv_d.at[c, s], device_id=peers[s], device_id_type=MESH)

    def ship(c):
        for s in range(n_head - 1):
            piece(c, s).start()

    unfilter_kernel(e, y, stats, all_sums, u, dx3, oc, cols_ref, ext_ref, pwi_ref, taps_ref, mixo_ref,
                    dx2_ref, do, pack_ref.at[pl.ds(layout.pointwise_in, layout.taps - layout.pointwise_in)], smalle, tapg, dyw, du, mask, prod, h3s, dgs, dms, gains2, live, n3, inv3, value3, gate3,
                    head_width=head_width, ship=ship, arrive=sums_in)
    own = pltpu.make_async_copy(do.at[me], do_all.at[me], local_d)
    own.start()
    end = put_taps(pack_ref, tapg[...], layout.taps)
    end = put_small(pack_ref, jnp.concatenate([smalld[...], smalle[...]], axis=0), end)
    if end < pack_ref.shape[0]:
        pack_ref[end:, :] = jnp.zeros((pack_ref.shape[0] - end, TILE), BF)
    own.wait()

    @pl.loop(0, rows // PIECE)
    def _(c):
        for s in range(n_head - 1):
            piece(c, s).wait()


def sum_scratch(count, n_tm, n_head):
    half = count // 2
    big = half // (n_tm // 2)
    shapes = [(half, TILE), (half, TILE), (n_tm // 2, big, TILE), (big, TILE), (n_head, big // n_head, TILE), (big, TILE), (half, TILE)]
    return [pltpu.VMEM(shape, BF) for shape in shapes]


def gradient_sum(src_ref, out_ref, first, scratch, sems, local, n_tm, n_head):
    got0, half, got1, part1, got2, part2, whole = scratch
    tm, head = lax.axis_index("tm"), lax.axis_index("head")
    n_chip = n_tm // 2
    chip, core = tm // 2, lax.rem(tm, 2)
    size = src_ref.shape[0] // 2
    big = size // n_chip
    small = big // n_head
    sibling = {"tm": chip * 2 + 1 - core}

    def rows(i, count, base=0):
        return pl.ds(pl.multiple_of(base + i * count, 16), count)

    def send(src, dst, phase, s, peer):
        return pltpu.make_async_remote_copy(src_ref=src, dst_ref=dst, send_sem=sems.at[2 * phase, s], recv_sem=sems.at[2 * phase + 1, s],
                                            device_id=peer, device_id_type=MESH)

    def chip_peer(s):
        return lax.rem(chip + s, n_chip)

    def head_peer(s):
        return lax.rem(head + s, n_head)

    def zero():
        return send(src_ref.at[rows(1 - core, size)], got0, 0, 0, sibling)

    def one(s):
        return send(half.at[rows(chip_peer(s), big)], got1.at[s], 1, s, {"tm": chip_peer(s) * 2 + core})

    def two(s):
        return send(part1.at[rows(head_peer(s), small)], got2.at[s], 2, s, {"head": head_peer(s)})

    def three(s):
        at = part2.at[rows(head, small)]
        return send(at, at, 3, s, {"head": head_peer(s)})

    def four(s):
        return send(part2, whole.at[rows(chip, big)], 4, s, {"tm": chip_peer(s) * 2 + core})

    def five():
        return send(whole, out_ref.at[rows(core, size, first)], 5, 0, sibling)

    def keep():
        return pltpu.make_async_copy(whole, out_ref.at[rows(core, size, first)], local)

    def added(got, n):
        total = got[0].astype(F32)
        for s in range(1, n):
            total = total + got[s].astype(F32)
        return total.astype(BF)

    def step0():
        zero().start()

    def step1():
        zero().wait()
        half[...] = (src_ref[rows(core, size), :].astype(F32) + got0[...].astype(F32)).astype(BF)
        pl.loop(1, n_chip)(lambda s: one(s).start())
        got1[0] = half[rows(chip, big), :]

    def step2():
        pl.loop(1, n_chip)(lambda s: one(s).wait())
        part1[...] = added(got1, n_chip)
        pl.loop(1, n_head)(lambda s: two(s).start())
        got2[0] = part1[rows(head, small), :]

    def step3():
        pl.loop(1, n_head)(lambda s: two(s).wait())
        part2[rows(head, small), :] = added(got2, n_head)
        pl.loop(1, n_head)(lambda s: three(s).start())

    def step4():
        pl.loop(1, n_head)(lambda s: three(s).wait())
        pl.loop(1, n_chip)(lambda s: four(s).start())
        whole[rows(chip, big), :] = part2[...]

    def step5():
        pl.loop(1, n_chip)(lambda s: four(s).wait())
        five().start()
        keep().start()

    def step6():
        keep().wait()
        five().wait()

    return step0, step1, step2, step3, step4, step5, step6


def final_kernel(*refs, n_tm, n_head, parts):
    dqkv_ref, sources, refs = refs[0], refs[1:11], refs[11:]
    (grad_ref, total_ref), loaded, refs = refs[:2], refs[2:12], refs[12:]
    early_ref, frames_ref, x1_ref, h2_ref, dx2_ref, dtab_ref, cols_ref, up_ref, down_ref, mix_ref = loaded
    (dqkv, late, h1s, das, s1s, dfs, dqs, gains, up_part, down_part, mix_part), refs = refs[:11], refs[11:]
    sum_refs = [refs[7 * i : 7 * i + 7] for i in range(3)]
    load_sems, send_q, recv_q, local_q, sum_sems, sum_local = refs[21:]
    me, peers, ids = head_peers(n_head)
    tm = lax.axis_index("tm")
    rows = x1_ref.shape[1]
    barrier = pltpu.get_barrier_semaphore()
    for peer in peers:
        pl.semaphore_signal(barrier, inc=1, device_id=peer, device_id_type=MESH)

    @pl.loop(1, n_tm)
    def _(s):
        pl.semaphore_signal(barrier, inc=1, device_id={"tm": lax.rem(tm + s, n_tm)}, device_id_type=MESH)

    loads = load_all(sources, loaded, load_sems)
    pl.semaphore_wait(barrier, n_head + n_tm - 2)

    def piece(c, s):
        at = pl.ds(pl.multiple_of(c * PIECE, PIECE), PIECE)
        return pltpu.make_async_remote_copy(src_ref=dqkv_ref.at[ids[s], :, at], dst_ref=dqkv.at[me, :, at], send_sem=send_q.at[c, s],
                                            recv_sem=recv_q.at[c, s], device_id=peers[s], device_id_type=MESH)

    @pl.loop(0, rows // PIECE)
    def _(c):
        for s in range(n_head - 1):
            piece(c, s).start()

    own = pltpu.make_async_copy(dqkv_ref.at[me], dqkv.at[me], local_q)
    own.start()
    for load in loads:
        load.wait()
    late_at, last_at, end = parts

    def summed(i, src, first):
        return gradient_sum(src, total_ref, first, sum_refs[i], sum_sems.at[i], sum_local.at[i], n_tm, n_head)

    early = summed(0, early_ref, 0)
    last = summed(2, late.at[pl.ds(last_at - late_at, end - last_at)], last_at)
    late_sum = summed(1, late.at[pl.ds(0, last_at - late_at)], late_at) if last_at > late_at else [lambda: None] * 7
    early[0]()
    early[1]()
    own.wait()

    def arrive(c):
        for s in range(n_head - 1):
            piece(c, s).wait()

    def between(c):
        pl.when(c == 0)(early[2])

    def mixed():
        early[3]()
        late_sum[0]()

    close_kernel(frames_ref, x1_ref, h2_ref, dx2_ref, dqkv, dtab_ref, cols_ref, up_ref, down_ref, mix_ref,
                 grad_ref, late, h1s, das, s1s, dfs, dqs, gains, up_part, down_part, mix_part, arrive=arrive, between=between, mixed=mixed)
    for step in (last[0], late_sum[1], last[1], late_sum[2], last[2], early[4], late_sum[3], last[3], late_sum[4], early[5], last[4],
                 late_sum[5], early[6], last[5], late_sum[6], last[6]):
        step()


VMEM_MIB = 62


def body(
    frames, lengths, first_gain, first_shift, first_up, first_up_bias, first_down, first_down_bias, mix_gain, mix_shift,
    mix_inputs, position_bias, mix_output, mix_output_bias, filter_gain, filter_shift, pointwise_in, pointwise_in_bias,
    depthwise_taps, batch_gain, batch_shift, pointwise_out, pointwise_out_bias, second_gain, second_shift, second_up,
    second_up_bias, second_down, second_down_bias, final_gain, final_shift, cotangent,
):
    weights = Weights(
        first_gain, first_shift, first_up, first_up_bias, first_down, first_down_bias, mix_gain, mix_shift, mix_inputs, position_bias,
        mix_output, mix_output_bias, filter_gain, filter_shift, pointwise_in, pointwise_in_bias, depthwise_taps, batch_gain,
        batch_shift, pointwise_out, pointwise_out_bias, second_gain, second_shift, second_up, second_up_bias, second_down,
        second_down_bias, final_gain, final_shift)
    rows, width = frames.shape
    hidden = first_up.shape[1]
    n_head, n_tm = lax.axis_size("head"), lax.axis_size("tm")
    heads, span = position_bias.shape
    head_width = width // heads
    packed_rows = -(-3 * head_width // 16) * 16
    group = rows * n_head
    lanes = rows + TILE
    slots = lengths.shape[1]
    taps = depthwise_taps.shape[0]
    layout = pack_layout(width, hidden, mix_inputs.shape[1], taps, n_tm * n_head)

    vectors = tuple(getattr(weights, name) for name in VEC.__dict__)
    frames_t, cot_t, first_down_t, second_down_t = frames.T, cotangent.T, first_down.T, second_down.T
    vm, dma, hbm = pltpu.VMEM, pltpu.SemaphoreType.DMA, pl.BlockSpec(memory_space=pl.ANY)
    steps = rows // PIECE
    piece_sems = dma((steps, n_head - 1))

    def comm_call(kernel, name, collective_id, ins, in_hbm, outs, out_hbm, scratch):
        return pl.pallas_call(
            kernel,
            out_shape=tuple(jax.ShapeDtypeStruct(s, t) for s, t in outs),
            in_specs=[hbm if i in in_hbm else pl.BlockSpec() for i in range(len(ins))],
            out_specs=tuple(hbm if i in out_hbm else pl.BlockSpec() for i in range(len(outs))),
            scratch_shapes=scratch,
            compiler_params=pltpu.CompilerParams(collective_id=collective_id, has_side_effects=True, vmem_limit_bytes=VMEM_MIB * 2**20),
            name=name,
        )(*ins)

    ins = (frames_t, lengths, first_up, first_down_t, mix_inputs) + vectors + (cot_t,)
    x1, h2, cols, bounds, plan, ext, qkv_all, x1l, x1r, cotl, cotr = comm_call(
        functools.partial(opening_kernel, packed_rows=packed_rows, n=n_head), "opening", 1, ins, (len(ins) - 1,),
        [((width, rows), F32), ((width, rows), BF), ((hidden, VEC_ROWS), F32), ((2, group + 2 * PAD), jnp.int32),
         ((group // BLK, 128), jnp.int32), ((1, lanes), jnp.int32), ((n_head, packed_rows, rows), BF),
         ((width, TILE), F32), ((width, TILE), F32), ((width, TILE), BF), ((width, TILE), BF)], range(6, 11),
        [vm((n_head, packed_rows, rows), BF), vm((1, group + 2 * TILE), jnp.int32), piece_sems, piece_sems, dma, dma((4,)), dma((4,))])
    o, of, lse = attend_forward(qkv_all, bounds, plan, position_bias, head_width)
    everyone_sems = dma((n_tm * n_head,))
    ins = (x1, x1l, x1r, cot_t, cotl, cotr, cols, ext, mix_output, pointwise_in, depthwise_taps, pointwise_out, second_up, second_down_t)
    out, dx2, do_all, pack = comm_call(
        functools.partial(middle_kernel, n_tm=n_tm, n_head=n_head, head_width=head_width, slot_count=slots, layout=layout),
        "middle", 2, (o,) + ins, range(len(ins) + 1),
        [((width, rows), BF), ((width, rows), F32), ((n_head, SLOT, rows), BF), ((layout.late, TILE), BF)],
        (2,),
        [vm(a.shape, a.dtype) for a in ins] + [
            vm((n_head, SLOT, rows + 2 * TILE), BF), vm((width, lanes), F32), vm((width + 16, rows), BF), vm((width, lanes), BF),
            vm((width, lanes), F32), vm((4, TILE), F32), vm((n_tm * n_head, 4, TILE), F32), vm((width, rows), F32),
            vm((width, lanes), F32), vm((4, TILE), F32), vm((n_tm * n_head, 4, TILE), F32), vm((n_head, SLOT, rows), BF),
            vm((width, lanes), F32), vm((taps + 1, 8, lanes), F32), vm((1, lanes), F32),
            vm((width, rows), BF), vm((hidden, rows), BF), vm((hidden + 16, rows), BF), vm((width, rows), BF),
            vm((width + 16, rows), BF), vm((width, rows), BF),
            vm((width, lanes), F32), vm((width, rows), F32), vm((taps, width, TILE), F32), vm((width + 16, rows), BF),
            vm((2 * width, rows), BF), vm((width, rows), BF), vm((2, width, TILE), F32),
            vm((16, 5 * TILE), F32), vm((16, 5 * TILE), F32), vm((taps, width), F32),
            vm((width, rows), F32), vm((1, rows), F32), vm((width, rows), F32), vm((width, rows), F32),
            dma((len(ins),)), dma((n_head - 1,)), dma((n_head - 1,)), dma, everyone_sems, everyone_sems, everyone_sems, everyone_sems,
            piece_sems, piece_sems, dma,
        ])
    dqkv, dtab = attend_backward(qkv_all, do_all, of, lse, bounds, plan, position_bias, head_width)
    parts = (layout.late, layout.last, layout.rows)
    sizes = (layout.late, max(layout.last - layout.late, 16 * n_tm * n_head), layout.rows - layout.last)
    ins = (pack, frames_t, x1, h2, dx2, dtab, cols, first_up, first_down_t, mix_inputs)
    grad, total = comm_call(
        functools.partial(final_kernel, n_tm=n_tm, n_head=n_head, parts=parts), "final", 3, (dqkv,) + ins, range(len(ins) + 1),
        [((width, rows), F32), ((layout.rows, TILE), BF)], (1,),
        [vm(a.shape, a.dtype) for a in ins] + [
            vm((n_head, packed_rows, rows), BF), vm((layout.rows - layout.late, TILE), BF),
            vm((width, rows), BF), vm((hidden, rows), BF), vm((hidden, rows), BF), vm((width, rows), BF),
            vm((n_head * packed_rows, rows), BF), vm((4, width, TILE), F32), vm((width, hidden), F32), vm((width, hidden), F32),
            vm((width, n_head * packed_rows), F32),
            *[s for size in sizes for s in sum_scratch(size, n_tm, n_head)],
            dma((len(ins),)), piece_sems, piece_sems, dma, dma((3, 12, max(n_tm // 2, n_head))), dma((3,)),
        ])
    shapes = Weights(**{n: w.shape for n, w in weights.__dict__.items()})
    shapes.first_down = shapes.second_down = first_down_t.shape
    results = [((width, rows), BF), ((width, rows), F32)] + [(s, F32) for s in shapes.__dict__.values()]
    out, grad, *summed = pl.pallas_call(
        functools.partial(unpack_kernel, layout=layout),
        out_shape=tuple(jax.ShapeDtypeStruct(s, t) for s, t in results),
        compiler_params=pltpu.CompilerParams(vmem_limit_bytes=VMEM_MIB * 2**20),
        name="unpack",
    )(total, out, grad)
    summed = Weights(*summed)
    summed.first_down, summed.second_down = summed.first_down.T, summed.second_down.T
    return (out.T, grad.T) + tuple(summed.__dict__.values())


def solution(mesh):
    rows = P(("tm", "head"), None)
    placed = (rows, P("tm", None)) + (P(),) * 29 + (rows,)
    return jax.shard_map(body, mesh=mesh, in_specs=placed, out_specs=(rows, rows) + (P(),) * 29, check_vma=False)
```

profile of v0, /device:TPU:0, one launch (start us, length us, event | category | flops | bytes accessed | tf_op | source)
XLA Modules:
  0.0 217.7 jit_solution(5259093463167072221)
XLA Ops:
  0.7 28.7 %opening.1 = (f32[144,1024]{1,0:T(8,128)}, bf16[144,1024]{1,0:T(8,128)(2,1)}, f32[576,24]{1,0:T(8,128)}, s32[2,6144]{1,0:T(2,128)}, s32[8,128]{1,0:T(8,128)}, /*...) custom-call(bf16[144,1024]{1,0:T(8,128)(2,1)} %bitcast.8, ...), custom_call_target="tpu_custom_call" | custom-call | tf_op jit(solution)/shard_map/opening/pallas_call | solution.py:1427
  29.4 29.3 %attend_forward.1 = (bf16[48,4352]{1,0:T(8,128)(2,1)}, f32[40,4096]{1,0:T(8,128)}, f32[1,4096]{1,0:T(1,128)}) custom-call(s32[8,128]{1,0:T(8,128)} %get-tuple-element.84.plan, bf16[4,112,1024]{2,1,0:T(8,128)(2,1)} %get-tuple-element.85.qkv_ref, bf16[4,128]{1,0:T(4,128)(2,1)} %table_ref.3, s32[2,6144]{1,0:T(2,128)} %get-tuple-element.86.bound_ref), custom_call_target="tpu_custom_call" | custom-call | tf_op jit(solution)/shard_map/attend_forward/pallas_call | solution.py:304
  58.7 56.6 %middle.1 = (bf16[144,1024]{1,0:T(8,128)(2,1)}, f32[144,1024]{1,0:T(8,128)}, bf16[4,48,1024]{2,1,0:T(8,128)(2,1)}, bf16[2560,128]{1,0:T(8,128)(2,1)}) custom-call(bf16[48,4352]{1,0:T(8,128)(2,1)} %get-tuple-element.87.refs_0_, f32[144,1024]{1,0:T(8,128)} %get-tuple-element.88.refs_1_.refs_3_, f32[144,128]{1,0:T(8,128)} %get-tuple-element.89.refs_2_, ...), custom_call_target="tpu_custom_call" | custom-call | tf_op jit(solution)/shard_map/middle/pallas_call | solution.py:1427
  115.3 51.7 %attend_backward.1 = (bf16[4,112,1024]{2,1,0:T(8,128)(2,1)}, f32[1,128]{1,0:T(1,128)}) custom-call(s32[8,128]{1,0:T(8,128)} %get-tuple-element.84.plan, bf16[4,112,1024]{2,1,0:T(8,128)(2,1)} %get-tuple-element.85.qkv_ref, bf16[4,48,1024]{2,1,0:T(8,128)(2,1)} %get-tuple-element.95.do_ref, f32[40,4096]{1,0:T(8,128)} %get-tuple-element.96.of_ref, ...), custom_call_target="tpu_custom_call" | custom-call | tf_op jit(solution)/shard_map/attend_backward/pallas_call | solution.py:467
  167.0 46.9 %final.1 = (f32[144,1024]{1,0:T(8,128)}, bf16[4608,128]{1,0:T(8,128)(2,1)}) custom-call(bf16[4,112,1024]{2,1,0:T(8,128)(2,1)} %get-tuple-element.98.refs_0_, bf16[2560,128]{1,0:T(8,128)(2,1)} %get-tuple-element.99.refs_1_, bf16[144,1024]{1,0:T(8,128)(2,1)} %bitcast.9, f32[144,1024]{1,0:T(8,128)} %get-tuple-element.88.refs_1_.refs_3_, ...), custom_call_target="tpu_custom_call" | custom-call | tf_op jit(solution)/shard_map/final/pallas_call | solution.py:1427
  213.9 3.3 %unpack.1 = (bf16[144,1024]{1,0:T(8,128)(2,1)}, f32[144,1024]{1,0:T(8,128)}, f32[144]{0:T(256)}, f32[144]{0:T(256)}, f32[144,576]{1,0:T(8,128)}, /*index=5*/f32[...) custom-call(bf16[4608,128]{1,0:T(8,128)(2,1)} %get-tuple-element.103, ...), custom_call_target="tpu_custom_call" | custom-call | tf_op jit(solution)/shard_map/unpack/pallas_call | solution.py:1484
where the time goes:
time: 222 us; the launch traced here: 218 us
  Pallas kernels  216 us (97%)
    pallas_call x3, Pallas kernels, comm_call(): pl.pallas_call(kernel, out_shape=tuple((jax.ShapeDtypeStruct(s, t) for s,...  132 us
    pallas_call x1, Pallas kernels, attend_backward(): pl.pallas_call(functools.partial(bwd_kernel, head_width=head_width), out_...  51.7 us
    pallas_call x1, Pallas kernels, attend_forward(): pl.pallas_call(functools.partial(fwd_kernel, head_width=head_width), out_...  29.3 us

commit v1 on v0

--- a/solution.py
+++ b/solution.py
@@ -19,6 +19,7 @@
 NEAR = PER + 2
 PAD = 8 * UNIT
 SLOT = 48
+MAIN = 32
 DEPTH = 128
 MASKED = -1e30
 GANG = 4
@@ -128,6 +129,15 @@
             far_windows(high, plain_high if whole else None, stop, functools.partial(step, part=part), after, True, fine)
 
 
+def fold_rows(four, pieces):
+    size = four.shape[1] // pieces
+    return jnp.concatenate([four[:, i * size : (i + 1) * size] for i in range(pieces)], axis=0)
+
+
+def unfold_rows(folded):
+    return jnp.concatenate([folded[i : i + 4, :] for i in range(0, folded.shape[0], 4)], axis=1)
+
+
 def part_at(block, part):
     if part is None:
         return units_at(PER * block, PER)
@@ -185,7 +195,7 @@
     return (key >= bounds[0:1, :] - first_key) & (key < bounds[1:2, :] - first_key)
 
 
-def fwd_kernel(plan, qkv_ref, table_ref, bound_ref, o_ref, of_ref, lse_ref, qaug, kn, vt, tile, top_ref, acc, *, head_width):
+def fwd_kernel(plan, qkv_ref, table_ref, bound_ref, o_ref, tail_ref, of_ref, lse_ref, qaug, kn, vt, tile, top_ref, acc, *, head_width):
     chunks, packed_rows, rows = qkv_ref.shape
     total = chunks * rows
     blocks = total // BLK
@@ -293,6 +303,7 @@
         total_p = acc[head_width : head_width + 1, at]
         out = acc[:, at] / total_p
         o_ref[:, pl.ds(pl.multiple_of(c * rows + UNIT, UNIT), rows)] = out.astype(BF)
+        tail_ref[c] = fold_rows(out[MAIN : MAIN + 4], 4).astype(BF)
         of_ref[:, at] = out[: of_ref.shape[0]]
         lse_ref[:, at] = lse_ref[:, at] + jnp.log2(total_p)
 
@@ -305,6 +316,7 @@
         functools.partial(fwd_kernel, head_width=head_width),
         out_shape=(
             jax.ShapeDtypeStruct((SLOT, total + 2 * UNIT), BF),
+            jax.ShapeDtypeStruct((chunks, 16, rows // 4), BF),
             jax.ShapeDtypeStruct((40, total), F32),
             jax.ShapeDtypeStruct((1, total), F32),
         ),
@@ -322,7 +334,7 @@
     )(plan, qkv, table, bounds)
 
 
-def bwd_kernel(plan, qkv_ref, do_ref, of_ref, lse_ref, table_ref, bound_ref, dqkv_ref, dtab_ref,
+def bwd_kernel(plan, qkv_ref, do_ref, tail_ref, of_ref, lse_ref, table_ref, bound_ref, dqkv_ref, dtab_ref,
                qaug, kn, kt, vn, dot_t, qn, don, tile, dq, band, ends, dv_acc, dk_acc, *, head_width):
     chunks, packed_rows, rows = qkv_ref.shape
     total = chunks * rows
@@ -362,9 +374,10 @@
         kn[at, :] = jnp.concatenate([k, k, one3], axis=0).T.astype(BF)
         kt[:, at] = k.astype(BF)
         vn[at, :] = jnp.concatenate([v, empty, one3], axis=0).T.astype(BF)
-        do = do_ref[c].astype(F32)
+        tail = unfold_rows(tail_ref[c].astype(F32))
+        do = jnp.concatenate([do_ref[c].astype(F32), tail, jnp.zeros((SLOT - MAIN - 4, rows), F32)], axis=0)
         centre = jnp.sum(do[: of_ref.shape[0]] * of_ref[:, at], axis=0, keepdims=True)
-        dot_t[:SLOT, at_pad] = do_ref[c]
+        dot_t[:SLOT, at_pad] = do.astype(BF)
         dot_t[SLOT : 2 * SLOT, at_pad] = empty.astype(BF)
         dot_t[2 * SLOT :, at_pad] = three_rows(-centre, rest).astype(BF)
         qn[at_pad, :] = jnp.concatenate([q + (row48 == head_width).astype(F32), empty, none], axis=0).T.astype(BF)
@@ -458,7 +471,7 @@
     dtab_ref[...] = out
 
 
-def attend_backward(qkv, do, of, lse, bounds, plan, table, head_width):
+def attend_backward(qkv, do, tail, of, lse, bounds, plan, table, head_width):
     chunks, packed_rows, rows = qkv.shape
     total = chunks * rows
     padded = total + 2 * PAD
@@ -470,7 +483,7 @@
             jax.ShapeDtypeStruct((chunks, packed_rows, rows), BF),
             jax.ShapeDtypeStruct((1, span), F32),
         ),
-        in_specs=[pl.BlockSpec(memory_space=pltpu.SMEM)] + [pl.BlockSpec()] * 6,
+        in_specs=[pl.BlockSpec(memory_space=pltpu.SMEM)] + [pl.BlockSpec()] * 7,
         scratch_shapes=[
             vm((3, DEPTH, padded), BF),
             vm((total, DEPTH), BF),
@@ -488,7 +501,7 @@
         ],
         compiler_params=pltpu.CompilerParams(vmem_limit_bytes=62 * 2**20),
         name="attend_backward",
-    )(plan, qkv, do, of, lse, table, bounds)
+    )(plan, qkv, do, tail, of, lse, table, bounds)
 
 VEC = types.SimpleNamespace(
     first_gain=0, first_shift=1, first_up_bias=2, first_down_bias=3, mix_gain=4, mix_shift=5, mix_output_bias=6, filter_gain=7,
@@ -604,6 +617,17 @@
     ext_ref[:, rows:] = jnp.where(iota((1, TILE), 1) < HALO, right, left)
 
 
+def split_heads(heads, head_width):
+    size = heads * head_width
+    row, column = iota((size, size), 0), iota((size, size), 1)
+    hit = jnp.zeros((size, size), jnp.bool_)
+    for h in range(heads):
+        f = column - head_width * h
+        mine = (f >= 0) & (f < head_width)
+        hit = hit | (mine & (f < MAIN) & (row == MAIN * h + f)) | (mine & (f >= MAIN) & (row == MAIN * heads + 4 * h + f - MAIN))
+    return hit.astype(F32).astype(BF)
+
+
 def conv_masks(mask_ref, ext_ref):
     seg = jnp.broadcast_to(ext_ref[...], (8, ext_ref.shape[1]))
     lanes = seg.shape[1]
@@ -612,7 +636,7 @@
         mask_ref[i] = (pltpu.roll(seg, (reach - i) % lanes, 1) == seg).astype(F32)
 
 
-def filter_kernel(x1_ref, x1l_ref, x1r_ref, o_ref, cols_ref, ext_ref, out_ref, pw_ref, taps_ref,
+def filter_kernel(x1_ref, x1l_ref, x1r_ref, o_ref, tail_ref, cols_ref, ext_ref, out_ref, pw_ref, taps_ref,
                   x2_ref, oc_ref, u_ref, y_ref, stat_ref, wide, mask, live_ref, h3s, n_ref, inv_ref, value_ref, gate_ref, *, head_width, slot_count, arrive):
     width, rows = x1_ref.shape
     lanes = rows + TILE
@@ -620,7 +644,7 @@
     taps = taps_ref.shape[0]
     out_t = flipped(out_ref[...])
     pw_t = flipped(pw_ref[...])
-    gather = spread_cols(width, heads, SLOT, head_width)
+    gather = split_heads(heads, head_width)
     seg = ext_ref[...]
     live = (seg >= 0) & (seg < slot_count)
     live_ref[...] = live.astype(F32)
@@ -635,8 +659,12 @@
         return jnp.concatenate([own, edge], axis=1)
 
     x1 = extended(x1_ref[...], x1l_ref[...], x1r_ref[...])
-    o = jnp.concatenate(
-        [extended(o_ref[h, :, TILE : TILE + rows], o_ref[h, :, :TILE], o_ref[h, :, TILE + rows :]) for h in range(heads)], axis=0)
+    main = [extended(o_ref[h, :MAIN, TILE : TILE + rows], o_ref[h, :MAIN, :TILE], o_ref[h, :MAIN, TILE + rows :]) for h in range(heads)]
+    tails = []
+    for h in range(heads):
+        left, right = (o_ref[h, MAIN:, at].astype(F32)[:4] for at in (slice(0, TILE), slice(TILE + rows, rows + 2 * TILE)))
+        tails.append(extended(unfold_rows(tail_ref[h].astype(F32)), left, right))
+    o = jnp.concatenate(main + [jnp.concatenate(tails, axis=0).astype(BF)], axis=0)
     oc = dot(gather, o, TN).astype(BF)
     x2 = x1 + (dot(out_t, oc) + col(cols_ref, VEC.mix_output_bias, width))
     n, inv = norm(x2)
@@ -788,13 +816,13 @@
 
 def unfilter_kernel(e_ref, y_ref, stats_ref, sums_ref, u_ref, dx3_ref, ocs, cols_ref, ext_ref, pw_ref, taps_ref,
                     out_ref, dx2_ref, do_ref, pack_ref, small_ref, tapg_ref,
-                    dyw, du_s, mask, prod, h3s, dgs, dms, gains, live_ref, n_ref, inv_ref, value_ref, gate_ref, *, head_width, ship, arrive):
+                    dyw, du_s, mask, prod, h3s, dgs, dms, gains, live_ref, n_ref, inv_ref, value_ref, gate_ref, tail_ref, *, head_width, ship, arrive):
     width, rows = dx3_ref.shape
     lanes = rows + TILE
     heads = do_ref.shape[0]
     taps = taps_ref.shape[0]
     tap_cols = taps_ref[...].astype(F32).T
-    out_w = dot(spread_cols(width, heads, SLOT, head_width), out_ref[...]).astype(BF)
+    out_w = dot(split_heads(heads, head_width), out_ref[...]).astype(BF)
     gains[...] = jnp.zeros_like(gains)
     fgain = col(cols_ref, VEC.filter_gain, width)
     mean, inv_b, count = total_stats(stats_ref, width)
@@ -831,15 +859,17 @@
         dx2 = dx3_ref[:, at] + norm_back(dh, n, inv, fgain)
         dx2_ref[:, at] = dx2
         dm = dx2.astype(BF)
-        do = dot(out_w, dm).astype(BF)
+        do = dot(out_w, dm)
         for h in range(heads):
-            do_ref[h, :, at] = do[h * SLOT : (h + 1) * SLOT]
+            do_ref[h, :, at] = do[h * MAIN : (h + 1) * MAIN].astype(BF)
+        tail_ref[:, at] = do[heads * MAIN :]
         ship(c)
         dgs[:, at] = dg
         dms[:, at] = dm
         for i, v in enumerate((dh * n, dh)):
             gains[i] += folded(v)
 
+    ship(rows // PIECE)
     whole = prod[...].reshape(taps * width, TILE)
     hi = whole.astype(BF)
     lo = (whole - hi.astype(F32)).astype(BF)
@@ -1156,14 +1186,14 @@
 
 
 def middle_kernel(*refs, n_tm, n_head, head_width, slot_count, layout):
-    o_ref, sources, refs = refs[0], refs[1:15], refs[15:]
-    (out_ref, dx2_ref, do_all, pack_ref), refs = refs[:4], refs[4:]
+    o_ref, o_tail, sources, refs = refs[0], refs[1], refs[2:16], refs[16:]
+    (out_ref, dx2_ref, do_all, do_tails, pack_ref), refs = refs[:5], refs[5:]
     loaded, refs = refs[:14], refs[14:]
     (x1_ref, x1l_ref, x1r_ref, cot_ref, cotl_ref, cotr_ref, cols_ref, ext_ref, mixo_ref, pwi_ref, taps_ref, pwo_ref, up_ref,
      down_ref) = loaded
     (o_own, x2, oc, u, y, stat, stats, dx3, e, sums, all_sums, do, wide, mask, live,
      h4s, das, s4s, dfs, ws, dcs, dyw, du, prod, h3s, dgs, dms, gains2, smalld, smalle, tapg,
-     n3, inv3, value3, gate3), refs = refs[:35], refs[35:]
+     n3, inv3, value3, gate3, tail_own, tail_wide, tail), refs = refs[:38], refs[38:]
     (load_sems, send_o, recv_o, local_o, send_a, recv_a, send_b, recv_b, send_d, recv_d, local_d) = refs
     me, peers, ids = head_peers(n_head)
     _, n, place = everyone(n_tm, n_head)
@@ -1177,27 +1207,36 @@
     loads = load_all(sources, loaded, load_sems)
     pl.semaphore_wait(barrier, n - 1)
 
-    def part(p):
-        return o_ref.at[:, pl.ds(pl.multiple_of(p * rows, TILE), rows + 2 * TILE)]
+    def parts(p):
+        first = pl.multiple_of(p * rows, TILE)
+        mine = o_own.at[me]
+        low, high = pl.ds(0, MAIN), pl.ds(MAIN, SLOT - MAIN)
+        left, right = pl.ds(0, TILE), pl.ds(rows + TILE, TILE)
+        return (
+            (o_ref.at[low, pl.ds(first, rows + 2 * TILE)], mine.at[low]),
+            (o_tail.at[p], tail_own.at[me]),
+            (o_ref.at[high, pl.ds(first, TILE)], mine.at[high, left]),
+            (o_ref.at[high, pl.ds(pl.multiple_of(first + rows + TILE, TILE), TILE)], mine.at[high, right]),
+        )
 
     copies = [
-        pltpu.make_async_remote_copy(src_ref=part(p), dst_ref=o_own.at[me], send_sem=send_o.at[s], recv_sem=recv_o.at[s],
+        pltpu.make_async_remote_copy(src_ref=src, dst_ref=dst, send_sem=send_o.at[s, i], recv_sem=recv_o.at[s, i],
                                      device_id=peer, device_id_type=MESH)
-        for s, (peer, p) in enumerate(zip(peers, ids))
+        for s, (peer, p) in enumerate(zip(peers, ids)) for i, (src, dst) in enumerate(parts(p))
     ]
     for copy in copies:
         copy.start()
-    own = pltpu.make_async_copy(part(me), o_own.at[me], local_o)
-    own.start()
+    own = [pltpu.make_async_copy(src, dst, local_o.at[i]) for i, (src, dst) in enumerate(parts(me))]
+    for copy in own:
+        copy.start()
     for load in loads:
         load.wait()
 
     def arrive():
-        own.wait()
-        for copy in copies:
+        for copy in own + copies:
             copy.wait()
 
-    filter_kernel(x1_ref, x1l_ref, x1r_ref, o_own, cols_ref, ext_ref, mixo_ref, pwi_ref, taps_ref, x2, oc, u, y, stat, wide, mask, live,
+    filter_kernel(x1_ref, x1l_ref, x1r_ref, o_own, tail_own, cols_ref, ext_ref, mixo_ref, pwi_ref, taps_ref, x2, oc, u, y, stat, wide, mask, live,
                   h3s, n3, inv3, value3, gate3, head_width=head_width, slot_count=slot_count, arrive=arrive)
     stats_out, stats_in = tell(stat, stats, send_a, recv_a, n_tm, n_head)
     sums_out, sums_in = tell(sums, all_sums, send_b, recv_b, n_tm, n_head)
@@ -1210,20 +1249,31 @@
         return pltpu.make_async_remote_copy(src_ref=do.at[ids[s], :, at], dst_ref=do_all.at[me, :, at], send_sem=send_d.at[c, s],
                                             recv_sem=recv_d.at[c, s], device_id=peers[s], device_id_type=MESH)
 
+    def ending(s):
+        return pltpu.make_async_remote_copy(src_ref=tail.at[ids[s]], dst_ref=do_tails.at[me], send_sem=send_d.at[rows // PIECE, s],
+                                            recv_sem=recv_d.at[rows // PIECE, s], device_id=peers[s], device_id_type=MESH)
+
     def ship(c):
+        if isinstance(c, int):
+            for h in range(n_head):
+                tail[h] = fold_rows(tail_wide[4 * h : 4 * h + 4, :], 4).astype(BF)
         for s in range(n_head - 1):
-            piece(c, s).start()
+            (ending(s) if isinstance(c, int) else piece(c, s)).start()
 
     unfilter_kernel(e, y, stats, all_sums, u, dx3, oc, cols_ref, ext_ref, pwi_ref, taps_ref, mixo_ref,
-                    dx2_ref, do, pack_ref.at[pl.ds(layout.pointwise_in, layout.taps - layout.pointwise_in)], smalle, tapg, dyw, du, mask, prod, h3s, dgs, dms, gains2, live, n3, inv3, value3, gate3,
+                    dx2_ref, do, pack_ref.at[pl.ds(layout.pointwise_in, layout.taps - layout.pointwise_in)], smalle, tapg, dyw, du, mask, prod, h3s, dgs, dms, gains2, live, n3, inv3, value3, gate3, tail_wide,
                     head_width=head_width, ship=ship, arrive=sums_in)
-    own = pltpu.make_async_copy(do.at[me], do_all.at[me], local_d)
-    own.start()
+    own = [pltpu.make_async_copy(do.at[me], do_all.at[me], local_d.at[0]), pltpu.make_async_copy(tail.at[me], do_tails.at[me], local_d.at[1])]
+    for copy in own:
+        copy.start()
     end = put_taps(pack_ref, tapg[...], layout.taps)
     end = put_small(pack_ref, jnp.concatenate([smalld[...], smalle[...]], axis=0), end)
     if end < pack_ref.shape[0]:
         pack_ref[end:, :] = jnp.zeros((pack_ref.shape[0] - end, TILE), BF)
-    own.wait()
+    for copy in own:
+        copy.wait()
+    for s in range(n_head - 1):
+        ending(s).wait()
 
     @pl.loop(0, rows // PIECE)
     def _(c):
@@ -1441,18 +1491,18 @@
          ((group // BLK, 128), jnp.int32), ((1, lanes), jnp.int32), ((n_head, packed_rows, rows), BF),
          ((width, TILE), F32), ((width, TILE), F32), ((width, TILE), BF), ((width, TILE), BF)], range(6, 11),
         [vm((n_head, packed_rows, rows), BF), vm((1, group + 2 * TILE), jnp.int32), piece_sems, piece_sems, dma, dma((4,)), dma((4,))])
-    o, of, lse = attend_forward(qkv_all, bounds, plan, position_bias, head_width)
+    o, o_tail, of, lse = attend_forward(qkv_all, bounds, plan, position_bias, head_width)
     everyone_sems = dma((n_tm * n_head,))
     ins = (x1, x1l, x1r, cot_t, cotl, cotr, cols, ext, mix_output, pointwise_in, depthwise_taps, pointwise_out, second_up, second_down_t)
-    out, dx2, do_all, pack = comm_call(
+    out, dx2, do_all, do_tails, pack = comm_call(
         functools.partial(middle_kernel, n_tm=n_tm, n_head=n_head, head_width=head_width, slot_count=slots, layout=layout),
-        "middle", 2, (o,) + ins, range(len(ins) + 1),
-        [((width, rows), BF), ((width, rows), F32), ((n_head, SLOT, rows), BF), ((layout.late, TILE), BF)],
-        (2,),
+        "middle", 2, (o, o_tail) + ins, range(len(ins) + 2),
+        [((width, rows), BF), ((width, rows), F32), ((n_head, MAIN, rows), BF), ((n_head, 16, rows // 4), BF), ((layout.late, TILE), BF)],
+        (2, 3),
         [vm(a.shape, a.dtype) for a in ins] + [
             vm((n_head, SLOT, rows + 2 * TILE), BF), vm((width, lanes), F32), vm((width + 16, rows), BF), vm((width, lanes), BF),
             vm((width, lanes), F32), vm((4, TILE), F32), vm((n_tm * n_head, 4, TILE), F32), vm((width, rows), F32),
-            vm((width, lanes), F32), vm((4, TILE), F32), vm((n_tm * n_head, 4, TILE), F32), vm((n_head, SLOT, rows), BF),
+            vm((width, lanes), F32), vm((4, TILE), F32), vm((n_tm * n_head, 4, TILE), F32), vm((n_head, MAIN, rows), BF),
             vm((width, lanes), F32), vm((taps + 1, 8, lanes), F32), vm((1, lanes), F32),
             vm((width, rows), BF), vm((hidden, rows), BF), vm((hidden + 16, rows), BF), vm((width, rows), BF),
             vm((width + 16, rows), BF), vm((width, rows), BF),
@@ -1460,10 +1510,11 @@
             vm((2 * width, rows), BF), vm((width, rows), BF), vm((2, width, TILE), F32),
             vm((16, 5 * TILE), F32), vm((16, 5 * TILE), F32), vm((taps, width), F32),
             vm((width, rows), F32), vm((1, rows), F32), vm((width, rows), F32), vm((width, rows), F32),
-            dma((len(ins),)), dma((n_head - 1,)), dma((n_head - 1,)), dma, everyone_sems, everyone_sems, everyone_sems, everyone_sems,
-            piece_sems, piece_sems, dma,
+            vm((n_head, 16, rows // 4), BF), vm((4 * n_head, rows), F32), vm((n_head, 16, rows // 4), BF),
+            dma((len(ins),)), dma((n_head - 1, 4)), dma((n_head - 1, 4)), dma((4,)), everyone_sems, everyone_sems, everyone_sems, everyone_sems,
+            dma((steps + 1, n_head - 1)), dma((steps + 1, n_head - 1)), dma((2,)),
         ])
-    dqkv, dtab = attend_backward(qkv_all, do_all, of, lse, bounds, plan, position_bias, head_width)
+    dqkv, dtab = attend_backward(qkv_all, do_all, do_tails, of, lse, bounds, plan, position_bias, head_width)
     parts = (layout.late, layout.last, layout.rows)
     sizes = (layout.late, max(layout.last - layout.late, 16 * n_tm * n_head), layout.rows - layout.last)
     ins = (pack, frames_t, x1, h2, dx2, dtab, cols, first_up, first_down_t, mix_inputs)

time: 222 us -> 218 us (0.982)
  Pallas kernels: 216 us -> 213 us
    pallas_call x3, Pallas kernels: 132 us -> 129 us  [comm_call(): pl.pallas_call(kernel, out_shape=tuple((jax.ShapeDtypeStruct(s, t) for s,...]
where the time goes in v1:
time: 218 us; the launch traced here: 214 us
  Pallas kernels  213 us (98%)
    pallas_call x3, Pallas kernels, comm_call(): pl.pallas_call(kernel, out_shape=tuple((jax.ShapeDtypeStruct(s, t) for s,...  129 us
    pallas_call x1, Pallas kernels, attend_backward(): pl.pallas_call(functools.partial(bwd_kernel, head_width=head_width), out_...  51.7 us
    pallas_call x1, Pallas kernels, attend_forward(): pl.pallas_call(functools.partial(fwd_kernel, head_width=head_width), out_...  29.3 us

profile of v1, /device:TPU:0, one launch (start us, length us, event | category | flops | bytes accessed | tf_op | source)
XLA Modules:
  0.0 214.0 jit_solution(2290266545348174580)
XLA Ops:
  0.7 28.7 %opening.1 = (f32[144,1024]{1,0:T(8,128)}, bf16[144,1024]{1,0:T(8,128)(2,1)}, f32[576,24]{1,0:T(8,128)}, s32[2,6144]{1,0:T(2,128)}, s32[8,128]{1,0:T(8,128)}, /*...) custom-call(bf16[144,1024]{1,0:T(8,128)(2,1)} %bitcast.8, ...), custom_call_target="tpu_custom_call" | custom-call | tf_op jit(solution)/shard_map/opening/pallas_call | solution.py:1477
  29.4 29.3 %attend_forward.1 = (bf16[48,4352]{1,0:T(8,128)(2,1)}, bf16[4,16,256]{2,1,0:T(8,128)(2,1)}, f32[40,4096]{1,0:T(8,128)}, f32[1,4096]{1,0:T(1,128)}) custom-call(s32[8,128]{1,0:T(8,128)} %get-tuple-element.86.plan, bf16[4,112,1024]{2,1,0:T(8,128)(2,1)} %get-tuple-element.87.qkv_ref, bf16[4,128]{1,0:T(4,128)(2,1)} %table_ref.3, ...), custom_call_target="tpu_custom_call" | custom-call | tf_op jit(solution)/shard_map/attend_forward/pallas_call | solution.py:315
  58.7 53.0 %middle.1 = (bf16[144,1024]{1,0:T(8,128)(2,1)}, f32[144,1024]{1,0:T(8,128)}, bf16[4,32,1024]{2,1,0:T(8,128)(2,1)}, bf16[4,16,256]{2,1,0:T(8,128)(2,1)}, bf16[2560,128]{1,0:T(8,128)(2,1)}) custom-call(bf16[48,4352]{1,0:T(8,128)(2,1)} %get-tuple-element.89.refs_0_, bf16[4,16,256]{2,1,0:T(8,128)(2,1)} %get-tuple-element.90.refs_1_, ...), custom_call_target="tpu_custom_call" | custom-call | tf_op jit(solution)/shard_map/middle/pallas_call | solution.py:1477
  111.7 51.7 %attend_backward.1 = (bf16[4,112,1024]{2,1,0:T(8,128)(2,1)}, f32[1,128]{1,0:T(1,128)}) custom-call(s32[8,128]{1,0:T(8,128)} %get-tuple-element.86.plan, bf16[4,112,1024]{2,1,0:T(8,128)(2,1)} %get-tuple-element.87.qkv_ref, bf16[4,32,1024]{2,1,0:T(8,128)(2,1)} %get-tuple-element.98.do_ref, bf16[4,16,256]{2,1,0:T(8,128)(2,1)} %get-tuple-element.99.tail_ref, ...), custom_call_target="tpu_custom_call" | custom-call | tf_op jit(solution)/shard_map/attend_backward/pallas_call | solution.py:480
  163.4 46.8 %final.1 = (f32[144,1024]{1,0:T(8,128)}, bf16[4608,128]{1,0:T(8,128)(2,1)}) custom-call(bf16[4,112,1024]{2,1,0:T(8,128)(2,1)} %get-tuple-element.102.refs_0_, bf16[2560,128]{1,0:T(8,128)(2,1)} %get-tuple-element.103.refs_1_, bf16[144,1024]{1,0:T(8,128)(2,1)} %bitcast.9, f32[144,1024]{1,0:T(8,128)} %get-tuple-element.91.refs_2_.refs_3_, ...), custom_call_target="tpu_custom_call" | custom-call | tf_op jit(solution)/shard_map/final/pallas_call | solution.py:1477
  210.3 3.3 %unpack.1 = (bf16[144,1024]{1,0:T(8,128)(2,1)}, f32[144,1024]{1,0:T(8,128)}, f32[144]{0:T(256)}, f32[144]{0:T(256)}, f32[144,576]{1,0:T(8,128)}, /*index=5*/f32[...) custom-call(bf16[4608,128]{1,0:T(8,128)(2,1)} %get-tuple-element.107, ...), custom_call_target="tpu_custom_call" | custom-call | tf_op jit(solution)/shard_map/unpack/pallas_call | solution.py:1535
